TPU v7x, 256 devices: a whole 4x4x8 slice. The times are simulated.
256 devices in a mesh: docs: 8 (over x, z_lo), cent: 32 (over z_hi, y, core).
Axes of the slice: x: 4, y: 4, z: 8 (z_hi: 4, z_lo: 2; z = z_hi * 2 + z_lo), core: 2. Of those that a mesh axis runs over, the one named last changes fastest.
Arguments:
- loader_blocks: bfloat16 [8, 32, 512, 384], P('docs', 'cent'), may hold values from -6 to 6
- block_counts: int32 [8, 32], P('docs', 'cent'), may hold values from 1 to 4, 64 in all within a row
- block_dest: int32 [8, 64], P('docs'), may hold values from 0 to 63, each once within a row
- centroids: bfloat16 [384, 16384], P(None, 'cent'), may hold values from -0.3125 to 0.3125
Outputs:
- centroid_sums: float32 [384, 16384], P('docs', 'cent')
- doc_weights: float32 [65536], P('docs')
Inputs may be any that keep to these rules, and one draw needn't show every extreme that they name: `block_counts`: each row sums to 64; every row has a host with exactly 4 live blocks. `block_dest`: each row is a permutation of 0 to 63.
All inputs are finite; a program needn't handle non-finite values.
Results may differ from a plain program's by a relative error of at most 0.0007.
The roundings to bfloat16 on the way count: a program that leaves them out, or rounds other values in their place, can miss the bound.
Values may be sent and summed in bfloat16 or wider, within the bound.
A program may use at most 64 MiB of HBM per device.

v0:
```python
import jax
import jax.numpy as jnp
from jax import lax
from jax.sharding import PartitionSpec as P

ROW_BLOCK = 128
ITERS = 2
SCORE_ROWS = 1024


SHARPNESS = 25.0


def unit_rows(rows):
    values = rows.astype(jnp.float32)
    factor = lax.rsqrt(jnp.mean(values * values, axis=-1, keepdims=True) + 1e-06)
    return (values * factor * values.shape[-1] ** (-0.5)).astype(jnp.bfloat16)


def unit_columns(weights):
    values = weights.astype(jnp.float32)
    factor = lax.rsqrt(jnp.mean(values * values, axis=0, keepdims=True) + 1e-06)
    return (values * factor * values.shape[0] ** (-0.5)).astype(jnp.bfloat16)


def invert_order(dest):
    count = dest.shape[0]
    where_p = jnp.arange(count, dtype=jnp.int32)
    return jnp.sum(jnp.where(dest[None, :] == where_p[:, None], where_p[None, :], 0), axis=1)


def source_slots(counts, dest, most):
    hosts = counts.shape[0]
    starts = (jnp.cumsum(counts) - counts).astype(jnp.int32)
    inverse = invert_order(dest)
    owner = jnp.sum((starts[None, :] <= inverse[:, None]).astype(jnp.int32), axis=1) - 1
    host_ids = jnp.arange(hosts, dtype=jnp.int32)
    begin = jnp.sum(jnp.where(host_ids[None, :] == owner[:, None], starts[None, :], 0), axis=1)
    return owner * most + (inverse - begin)


def column_scale(partial_value, total_cent):
    column_sum = lax.psum(partial_value, "docs")
    return 1.0 / (total_cent * column_sum)


def on_device(loader_blocks, block_counts, block_dest, centroids):
    width = loader_blocks.shape[3]
    most = loader_blocks.shape[2] // ROW_BLOCK
    dest = block_dest[0]
    blocks = dest.shape[0]
    gathered, counts = (
        lax.all_gather(loader_blocks, "cent", axis=1, tiled=True),
        lax.all_gather(block_counts, "cent", axis=1, tiled=True),
    )
    flat = source_slots(counts[0], dest, most)
    pool = gathered.reshape(-1, ROW_BLOCK, width)
    rows = pool[flat].reshape(blocks * ROW_BLOCK, width)
    unit_docs = unit_rows(rows)
    unit_cents = unit_columns(centroids)
    local_rows = unit_docs.shape[0]
    columns = unit_cents.shape[1]
    all_docs = local_rows * lax.axis_size("docs")
    total_cent = columns * lax.axis_size("cent")
    tiles = unit_docs.reshape(local_rows // SCORE_ROWS, SCORE_ROWS, width)

    def kernel(tile):
        return jnp.exp(SHARPNESS * jnp.dot(tile, unit_cents, preferred_element_type=jnp.float32))

    def first_step(carry, tile):
        return (carry + jnp.sum(kernel(tile), axis=0), None)

    partial_value, _ = lax.scan(first_step, jnp.zeros((columns,), jnp.float32), tiles)
    cent_scale = column_scale(partial_value, total_cent)
    numer_zero = jnp.zeros((width, columns), jnp.float32)
    column_zero = jnp.zeros((columns,), jnp.float32)

    def finish(carry, tile, weights, doc_scale, scale_now, last):
        if last:
            plan = (all_docs * doc_scale[:, None] * weights * scale_now[None, :]).astype(
                jnp.bfloat16
            )
            return carry + lax.dot_general(
                tile, plan, (((0,), (0,)), ((), ())), preferred_element_type=jnp.float32
            )
        return carry + jnp.sum(doc_scale[:, None] * weights, axis=0)

    for turn in range(ITERS):
        last = turn + 1 == ITERS
        start_carry = numer_zero if last else column_zero
        scale_now = cent_scale

        def sweep(carry, tile):
            weights = kernel(tile)
            row_part = jnp.sum(weights * scale_now[None, :], axis=1)
            row_sum = lax.psum(row_part, "cent")
            doc_scale = 1.0 / (all_docs * row_sum)
            return (finish(carry, tile, weights, doc_scale, scale_now, last), doc_scale)

        result, doc_scales = lax.scan(sweep, start_carry, tiles)
        if last:
            numer = result
            doc_weights = jnp.log(all_docs * doc_scales.reshape(local_rows))
        else:
            cent_scale = column_scale(result, total_cent)
    return (lax.psum_scatter(numer, "docs", scatter_dimension=0, tiled=True), doc_weights)


def solution(mesh):
    in_specs = (P("docs", "cent", None, None), P("docs", "cent"), P("docs", None), P(None, "cent"))
    out_specs = (P("docs", "cent"), P("docs"))
    return jax.shard_map(
        on_device, mesh=mesh, in_specs=in_specs, out_specs=out_specs, check_vma=False
    )
```

profile of v0, /device:TPU:1, one launch (start us, length us, event | category | flops | bytes accessed | tf_op | source)
XLA Modules:
  0.0 1401.4 jit_solution(3173681838368494547)
XLA Ops:
  10.6 18.9 %all-reduce = s32[32]{0:T(128)S(1)} all-reduce(s32[32]{0:T(128)S(1)} %bitcast_dynamic-update-slice_fusion), channel_id=1, replica_groups=mesh['docs'=8,'cent'=32] {'cent'}, use_global_device_ids=true, to_apply=%add | all-reduce | flops 32 | bytes 256
  32.9 74.1 %all-gather.2.cloned.1.call-done = bf16[1,32,512,384]{3,2,0,1:T(8,128)(2,1)} async-done(((bf16[1,1,512,384]{3,2,0,1:T(8,128)(2,1)}), bf16[1,32,512,384]{3,2,0,1:T(8,128)(2,1)}) %all-gather.2.cloned.1.call-update) | async-done | bytes 12582928 | tf_op jit(solution)/shard_map/all_gather | solution.py:53
  134.7 15.2 %while.35 = (s32[]{:T(128)}, f32[512]{0:T(512)S(1)}, bf16[8,1024,384]{2,1,0:T(8,128)(2,1)}, bf16[384,512]{1,0:T(8,128)(2,1)S(1)}, s32[]{:T(128)}, /*index=5*/s32[]{:T(128)}) while((s32[]{:T(128)}, f32[512]{0:T(512)S(1)}, bf16[8,1024,384]{2,1,0:T(8,128)(2,1)}, bf16[384,512]{1,0:T(8,128)(2,1)S(1)}, s32[]{:T(128)}, ...), condition=%wide.region_8.9_spmd.clone, body=%wide.region_6.8_spmd.clone.sunk | while | flops 403702272 | bytes 1188431 | solution.py:73
  149.9 22.0 %psum.28 = f32[512]{0:T(512)S(1)} all-reduce(f32[512]{0:T(512)S(1)} %get-tuple-element.84), channel_id=1, replica_groups=mesh['docs'=8,'cent'=32] {'docs'}, use_global_device_ids=true, to_apply=%region_9.10 | all-reduce | flops 512 | bytes 4096 | tf_op jit(solution)/shard_map/psum | solution.py:43
  171.9 581.8 %while.36 = (s32[]{:T(128)}, f32[512]{0:T(512)S(1)}, bf16[8,1024,384]{2,1,0:T(8,128)(2,1)}, bf16[384,512]{1,0:T(8,128)(2,1)S(1)}, f32[512]{0:T(512)S(1)}, /*index=5*/s32[]{:T(128)}, s32[]{:T(128)}) while((s32[]{:T(128)}, f32[512]{0:T(512)S(1)}, bf16[8,1024,384]{2,1,0:T(8,128)(2,1)}, bf16[384,512]{1,0:T(8,128)(2,1)S(1)}, ...), condition=%wide.region_14.15_spmd.clone, body=%wide.region_10.14_spmd.clone.sunk | while | flops 405801472 | bytes 5409367 | solution.py:100
  173.9 73.2 %psum.34 = f32[1024]{0:T(1024)S(1)} all-reduce(f32[1024]{0:T(1024)S(1)} %get-tuple-element.272), channel_id=1, replica_groups=mesh['docs'=8,'cent'=32] {'cent'}, use_global_device_ids=true, to_apply=%region_12.12 | all-reduce | flops 1024 | bytes 8192 | tf_op jit(solution)/shard_map/while/body/eval_jaxpr/psum | solution.py:96
  249.5 69.9 %psum.34 = f32[1024]{0:T(1024)S(1)} all-reduce(f32[1024]{0:T(1024)S(1)} %get-tuple-element.272), channel_id=1, replica_groups=mesh['docs'=8,'cent'=32] {'cent'}, use_global_device_ids=true, to_apply=%region_12.12 | all-reduce | flops 1024 | bytes 8192 | tf_op jit(solution)/shard_map/while/body/eval_jaxpr/psum | solution.py:96
  321.8 69.9 %psum.34 = f32[1024]{0:T(1024)S(1)} all-reduce(f32[1024]{0:T(1024)S(1)} %get-tuple-element.272), channel_id=1, replica_groups=mesh['docs'=8,'cent'=32] {'cent'}, use_global_device_ids=true, to_apply=%region_12.12 | all-reduce | flops 1024 | bytes 8192 | tf_op jit(solution)/shard_map/while/body/eval_jaxpr/psum | solution.py:96
  394.1 69.9 %psum.34 = f32[1024]{0:T(1024)S(1)} all-reduce(f32[1024]{0:T(1024)S(1)} %get-tuple-element.272), channel_id=1, replica_groups=mesh['docs'=8,'cent'=32] {'cent'}, use_global_device_ids=true, to_apply=%region_12.12 | all-reduce | flops 1024 | bytes 8192 | tf_op jit(solution)/shard_map/while/body/eval_jaxpr/psum | solution.py:96
  466.4 69.9 %psum.34 = f32[1024]{0:T(1024)S(1)} all-reduce(f32[1024]{0:T(1024)S(1)} %get-tuple-element.272), channel_id=1, replica_groups=mesh['docs'=8,'cent'=32] {'cent'}, use_global_device_ids=true, to_apply=%region_12.12 | all-reduce | flops 1024 | bytes 8192 | tf_op jit(solution)/shard_map/while/body/eval_jaxpr/psum | solution.py:96
  538.7 69.9 %psum.34 = f32[1024]{0:T(1024)S(1)} all-reduce(f32[1024]{0:T(1024)S(1)} %get-tuple-element.272), channel_id=1, replica_groups=mesh['docs'=8,'cent'=32] {'cent'}, use_global_device_ids=true, to_apply=%region_12.12 | all-reduce | flops 1024 | bytes 8192 | tf_op jit(solution)/shard_map/while/body/eval_jaxpr/psum | solution.py:96
  611.0 69.9 %psum.34 = f32[1024]{0:T(1024)S(1)} all-reduce(f32[1024]{0:T(1024)S(1)} %get-tuple-element.272), channel_id=1, replica_groups=mesh['docs'=8,'cent'=32] {'cent'}, use_global_device_ids=true, to_apply=%region_12.12 | all-reduce | flops 1024 | bytes 8192 | tf_op jit(solution)/shard_map/while/body/eval_jaxpr/psum | solution.py:96
  683.3 70.0 %psum.34 = f32[1024]{0:T(1024)S(1)} all-reduce(f32[1024]{0:T(1024)S(1)} %get-tuple-element.272), channel_id=1, replica_groups=mesh['docs'=8,'cent'=32] {'cent'}, use_global_device_ids=true, to_apply=%region_12.12 | all-reduce | flops 1024 | bytes 8192 | tf_op jit(solution)/shard_map/while/body/eval_jaxpr/psum | solution.py:96
  753.7 12.9 psum.29
  766.6 595.3 %while.37 = (s32[]{:T(128)}, f32[384,512]{1,0:T(8,128)S(1)}, f32[8,1024]{1,0:T(8,128)S(1)}, bf16[8,1024,384]{2,1,0:T(8,128)(2,1)}, bf16[384,512]{1,0:T(8,128)(2,...) while((s32[]{:T(128)}, f32[384,512]{1,0:T(8,128)S(1)}, f32[8,1024]{1,0:T(8,128)S(1)}, ...), condition=%wide.region_19.20_spmd.clone, body=%wide.region_16.19_spmd.clone.sunk | while | flops 809372672 | bytes 7775331 | solution.py:100
  768.6 73.0 %psum.35 = f32[1024]{0:T(1024)S(1)} all-reduce(f32[1024]{0:T(1024)S(1)} %get-tuple-element.280), channel_id=1, replica_groups=mesh['docs'=8,'cent'=32] {'cent'}, use_global_device_ids=true, to_apply=%region_18.18 | all-reduce | flops 1024 | bytes 8192 | tf_op jit(solution)/shard_map/while/body/eval_jaxpr/psum | solution.py:96
  845.7 69.9 %psum.35 = f32[1024]{0:T(1024)S(1)} all-reduce(f32[1024]{0:T(1024)S(1)} %get-tuple-element.280), channel_id=1, replica_groups=mesh['docs'=8,'cent'=32] {'cent'}, use_global_device_ids=true, to_apply=%region_18.18 | all-reduce | flops 1024 | bytes 8192 | tf_op jit(solution)/shard_map/while/body/eval_jaxpr/psum | solution.py:96
  919.7 69.9 %psum.35 = f32[1024]{0:T(1024)S(1)} all-reduce(f32[1024]{0:T(1024)S(1)} %get-tuple-element.280), channel_id=1, replica_groups=mesh['docs'=8,'cent'=32] {'cent'}, use_global_device_ids=true, to_apply=%region_18.18 | all-reduce | flops 1024 | bytes 8192 | tf_op jit(solution)/shard_map/while/body/eval_jaxpr/psum | solution.py:96
  993.7 69.9 %psum.35 = f32[1024]{0:T(1024)S(1)} all-reduce(f32[1024]{0:T(1024)S(1)} %get-tuple-element.280), channel_id=1, replica_groups=mesh['docs'=8,'cent'=32] {'cent'}, use_global_device_ids=true, to_apply=%region_18.18 | all-reduce | flops 1024 | bytes 8192 | tf_op jit(solution)/shard_map/while/body/eval_jaxpr/psum | solution.py:96
  1067.7 69.9 %psum.35 = f32[1024]{0:T(1024)S(1)} all-reduce(f32[1024]{0:T(1024)S(1)} %get-tuple-element.280), channel_id=1, replica_groups=mesh['docs'=8,'cent'=32] {'cent'}, use_global_device_ids=true, to_apply=%region_18.18 | all-reduce | flops 1024 | bytes 8192 | tf_op jit(solution)/shard_map/while/body/eval_jaxpr/psum | solution.py:96
  1141.8 69.9 %psum.35 = f32[1024]{0:T(1024)S(1)} all-reduce(f32[1024]{0:T(1024)S(1)} %get-tuple-element.280), channel_id=1, replica_groups=mesh['docs'=8,'cent'=32] {'cent'}, use_global_device_ids=true, to_apply=%region_18.18 | all-reduce | flops 1024 | bytes 8192 | tf_op jit(solution)/shard_map/while/body/eval_jaxpr/psum | solution.py:96
  1215.8 69.9 %psum.35 = f32[1024]{0:T(1024)S(1)} all-reduce(f32[1024]{0:T(1024)S(1)} %get-tuple-element.280), channel_id=1, replica_groups=mesh['docs'=8,'cent'=32] {'cent'}, use_global_device_ids=true, to_apply=%region_18.18 | all-reduce | flops 1024 | bytes 8192 | tf_op jit(solution)/shard_map/while/body/eval_jaxpr/psum | solution.py:96
  1289.8 69.9 %psum.35 = f32[1024]{0:T(1024)S(1)} all-reduce(f32[1024]{0:T(1024)S(1)} %get-tuple-element.280), channel_id=1, replica_groups=mesh['docs'=8,'cent'=32] {'cent'}, use_global_device_ids=true, to_apply=%region_18.18 | all-reduce | flops 1024 | bytes 8192 | tf_op jit(solution)/shard_map/while/body/eval_jaxpr/psum | solution.py:96
  1363.4 31.2 %reduce-scatter.2.cloned.1.call-done = f32[48,512]{1,0:T(8,128)} async-done(((f32[384,512]{1,0:T(8,128)}), f32[48,512]{1,0:T(8,128)}) %reduce-scatter.2.cloned.1.call-update) | async-done | bytes 98320 | tf_op jit(solution)/shard_map/reduce_scatter | solution.py:106
  (116 shorter events, 102.1 us)
Async XLA Ops:
  7.2 99.8 %all-gather.2.cloned.1.call-start = ((), (), s32[]{:S(2)}) async-start(), calls=%async_computation.1 | async-start | bytes 12976128 | tf_op jit(solution)/shard_map/all_gather | solution.py:53
  7.9 1386.7 %reduce-scatter.2.cloned.1.call-start = ((), (), s32[]{:S(2)}) async-start(), calls=%async_computation.2 | async-start | bytes 884736 | tf_op jit(solution)/shard_map/reduce_scatter | solution.py:106
  115.6 9.2 copy-start
  1361.8 0.9 copy-start.1
Sparse Core Ops, SparseCore 0:
  10.5 96.4 all-gather.1
  1362.9 31.6 reduce-scatter.1
where the time goes:
time: 1410 us; the launch traced here: 1400 us
  blocking collectives  1180 us (84%)
  waiting for transfers between devices  106 us (8%)
  matrix products  62.6 us (4%)
  other arithmetic  25.8 us (2%)
  between operations  14.8 us (1%)
    psum x16, blocking collectives, sweep(): row_sum = lax.psum(row_part, 'cent')  1120 us
    all_gather x1, waiting for transfers between devices, on_device(): lax.all_gather(loader_blocks, 'cent', axis=1, tiled=True)  74.1 us
    dot_general x24, matrix products, kernel(): jnp.dot(tile, unit_cents, preferred_element_type=jnp.float32)  46.6 us
    psum x2, blocking collectives, column_scale(): column_sum = lax.psum(partial_value, 'docs')  34.9 us
    reduce_scatter x1, waiting for transfers between devices, on_device(): lax.psum_scatter(numer, 'docs', scatter_dimension=0, tiled=True)  31.2 us
  transfers between devices with their start and end apart: 2, of which 2 were waited for; matrix products, arithmetic and copies ran while one was open for 0% of the time, Pallas kernels for 0%

commit v1 on v0

v1 whole, which is shorter than its diff:
```python
import jax
import jax.numpy as jnp
from jax import lax
from jax.experimental import pallas as pl
from jax.experimental.pallas import tpu as pltpu
from jax.sharding import PartitionSpec as P

F32 = jnp.float32
BF16 = jnp.bfloat16

WIDTH = 384
COLS = 512
SLOTS = 512
BLOCK = 128
MOST = 4
HOSTS = 8
BLOCKS = HOSTS * MOST
QUARTERS = 4
SHARPNESS = 25.0
DOCS = 65536.0
CENTROIDS = 16384.0


def mod(value, size):
    return lax.rem(value, jnp.int32(size))


def wide(tile):
    return jnp.concatenate([tile] * (COLS // BLOCK), axis=1)


def device(x, y, z, core):
    return (x * 2 + mod(z, 2), (lax.div(z, jnp.int32(2)) * 4 + y) * 2 + core)


def kernel(
    docs_ref,
    counts_ref,
    dest_ref,
    cents_ref,
    numer_out,
    weights_out,
    units,
    units_t,
    cents,
    score,
    live_counts,
    live,
    col_acc,
    col_x,
    col_z,
    scale,
    rows,
    doc_row,
    doc_col,
    numer,
    far,
    near,
    reduced,
    shares,
    doc_log,
    unit_send,
    unit_recv,
    cent_send,
    cent_recv,
    count_send,
    count_recv,
    colx_send,
    colx_recv,
    colz_send,
    colz_recv,
    row_send,
    row_recv,
    log_send,
    log_recv,
    sum_send,
    sum_recv,
    share_send,
    share_recv,
):
    doc_index = lax.axis_index("docs")
    cent_index = lax.axis_index("cent")
    x = lax.div(doc_index, jnp.int32(2))
    lo = mod(doc_index, 2)
    core = mod(cent_index, 2)
    y = mod(lax.div(cent_index, jnp.int32(2)), 4)
    hi = lax.div(cent_index, jnp.int32(8))
    z = hi * 2 + lo
    host = y * 2 + core

    def along_host(step):
        other = mod(host + step, HOSTS)
        return device(x, lax.div(other, jnp.int32(2)), z, mod(other, 2))

    def along_x(step):
        return device(mod(x + step, 4), y, z, core)

    def along_z(step):
        return device(x, y, mod(z + step, 8), core)

    def along_y(step):
        return device(x, mod(y + step, 4), z, core)

    def remote(src, dst, send, recv, target):
        return pltpu.make_async_remote_copy(
            src_ref=src,
            dst_ref=dst,
            send_sem=send,
            recv_sem=recv,
            device_id=target,
            device_id_type=pl.DeviceIdType.MESH,
        )

    barrier = pltpu.get_barrier_semaphore()
    for step in range(1, 8):
        pl.semaphore_signal(
            barrier, inc=1, device_id=along_host(step), device_id_type=pl.DeviceIdType.MESH
        )
        pl.semaphore_signal(
            barrier, inc=1, device_id=along_z(step), device_id_type=pl.DeviceIdType.MESH
        )
    for step in range(1, 4):
        pl.semaphore_signal(
            barrier, inc=1, device_id=along_x(step), device_id_type=pl.DeviceIdType.MESH
        )

    values = docs_ref[...].astype(F32)
    factor = lax.rsqrt(jnp.mean(values * values, axis=1, keepdims=True) + 1e-06)
    units[host] = (values * factor * WIDTH ** (-0.5)).astype(BF16)
    values = cents_ref[...].astype(F32)
    factor = lax.rsqrt(jnp.mean(values * values, axis=0, keepdims=True) + 1e-06)
    cents[hi] = (values * factor * WIDTH ** (-0.5)).astype(BF16)
    live_counts[host] = jnp.full((8, BLOCK), counts_ref[0, 0].astype(F32), F32)
    col_acc[...] = jnp.zeros_like(col_acc)

    pl.semaphore_wait(barrier, 17)

    left_y, right_y, far_y = mod(y + 3, 4), mod(y + 1, 4), mod(y + 2, 4)
    first, second, whole = pl.ds(0, SLOTS // 2), pl.ds(SLOTS // 2, SLOTS // 2), pl.ds(0, SLOTS)
    to_right, to_left = along_y(1), along_y(3)
    to_twin = device(x, y, z, 1 - core)
    own, from_left, from_right, across = (
        host,
        left_y * 2 + core,
        right_y * 2 + core,
        far_y * 2 + core,
    )
    unit_plan = [
        (own, first, to_right),
        (own, second, to_right),
        (own, first, to_left),
        (own, second, to_left),
        (from_left, first, to_right),
        (from_right, second, to_left),
        (own, whole, to_twin),
        (from_left, first, to_twin),
        (from_left, second, to_twin),
        (from_right, first, to_twin),
        (from_right, second, to_twin),
        (across, first, to_twin),
        (across, second, to_twin),
    ]
    unit_copies = []
    for at, (which, part, target) in enumerate(unit_plan):
        ref = units.at[which, part]
        unit_copies.append(remote(ref, ref, unit_send.at[at], unit_recv.at[at], target))

    chunk = WIDTH // 4
    rising, falling = [], []
    for step in range(6):
        back = 1 if step < 4 else 2
        which = mod(hi - back + lo + 4, QUARTERS)
        ref = cents.at[which, pl.ds((step % 4) * chunk, chunk)]
        rising.append(remote(ref, ref, cent_send.at[step], cent_recv.at[step], along_z(1)))
        ahead = 0 if step < 4 else 1
        which = mod(hi + ahead + lo, QUARTERS)
        ref = cents.at[which, pl.ds(((step + 2) % 4) * chunk, chunk)]
        falling.append(
            remote(ref, ref, cent_send.at[6 + step], cent_recv.at[6 + step], along_z(7))
        )

    def cent_open():
        @pl.when(lo == 1)
        def _():
            for step in range(4):
                rising[step].start()

        @pl.when(lo == 0)
        def _():
            for step in range(4):
                falling[step].start()

    def cent_start(step):
        @pl.when(lo == 1)
        def _():
            if step >= 4:
                rising[step - 4].wait_recv()
                rising[step].start()
            falling[step].wait_recv()
            falling[step].start()

        @pl.when(lo == 0)
        def _():
            if step >= 4:
                falling[step - 4].wait_recv()
                falling[step].start()
            rising[step].wait_recv()
            rising[step].start()

    def cent_finish():
        @pl.when(lo == 1)
        def _():
            for step in range(2, 6):
                rising[step].wait_recv()

        @pl.when(lo == 0)
        def _():
            for step in range(2, 6):
                falling[step].wait_recv()

    count_copies = [
        remote(
            live_counts.at[host],
            live_counts.at[host],
            count_send.at[step - 1],
            count_recv.at[step - 1],
            along_host(step),
        )
        for step in range(1, 8)
    ]
    for at in (0, 3, 1, 2, 6):
        unit_copies[at].start()
    for copy in count_copies:
        copy.start()
    cent_open()

    def score_tile(turn_y, flip, turn_z):
        which = mod(y + (turn_y ^ (turn_y >> 1)), 4) * 2 + (core ^ flip)
        quarter = mod(hi + (turn_z ^ (turn_z >> 1)), QUARTERS)
        logits = jnp.dot(units[which], cents[quarter], preferred_element_type=F32)
        weights = jnp.exp(SHARPNESS * logits)
        score[quarter, pl.ds(pl.multiple_of(which * SLOTS, SLOTS), SLOTS), :] = weights
        total = col_acc[quarter]
        for slot in range(MOST):
            part = weights[slot * BLOCK : (slot + 1) * BLOCK]
            part = jnp.sum(part.reshape(BLOCK // 8, 8, COLS), axis=0)
            here = jnp.where(live_counts[which] > slot, 1.0, 0.0)
            total = total + part * wide(here)
        col_acc[quarter] = total

    def score_tiles(turns_y, turns_z):
        (y_from, y_to), (z_from, z_to) = turns_y, turns_z
        wide_z = z_to - z_from

        def body(at, _):
            turn_z = z_from + lax.rem(at, wide_z)
            rest = lax.div(at, wide_z)
            score_tile(y_from + (rest >> 1), rest & 1, turn_z)
            return 0

        lax.fori_loop(0, (y_to - y_from) * 2 * wide_z, body, 0)

    for copy in count_copies:
        copy.wait_recv()
    cent_start(0)
    unit_copies[0].wait_recv()
    unit_copies[4].start()
    unit_copies[7].start()
    unit_copies[3].wait_recv()
    unit_copies[5].start()
    unit_copies[10].start()
    cent_start(1)
    unit_copies[6].wait_recv()
    score_tiles((0, 1), (0, 1))
    cent_start(2)
    cent_start(3)
    for at in (1, 2):
        unit_copies[at].wait_recv()
    for at in (8, 9):
        unit_copies[at].start()
    cent_start(4)
    cent_start(5)
    for at in (7, 8, 9, 10):
        unit_copies[at].wait_recv()
    score_tiles((1, 3), (0, 1))
    for at in (4, 5):
        unit_copies[at].wait_recv()
    for at in (11, 12):
        unit_copies[at].start()
    cent_finish()
    score_tiles((0, 3), (1, 4))
    for at in (11, 12):
        unit_copies[at].wait_recv()
    score_tiles((3, 4), (0, 4))

    for at in range(13):
        unit_copies[at].wait_send()
    for step in range(6):
        rising[step].wait_send()
        falling[step].wait_send()
    for copy in count_copies:
        copy.wait_send()

    for which in range(HOSTS):
        units_t[which] = units[which].T
        for slot in range(MOST):
            at = which * MOST + slot
            live[at : at + 1, :] = jnp.where(live_counts[which, 0:1, :] > slot, 1.0, 0.0)

    def exchange_columns(turn):
        for quarter in range(QUARTERS):
            total = jnp.sum(col_acc[quarter], axis=0, keepdims=True)
            for part in range(2):
                col_x[turn, x, 2 * quarter + part : 2 * quarter + part + 1, :] = total[
                    :, part * 256 : (part + 1) * 256
                ]
        copies = [
            remote(
                col_x.at[turn, x],
                col_x.at[turn, x],
                colx_send.at[turn * 3 + step - 1],
                colx_recv.at[turn * 3 + step - 1],
                along_x(step),
            )
            for step in range(1, 4)
        ]
        for copy in copies:
            copy.start()
        for copy in copies:
            copy.wait()
        col_z[turn, z] = (col_x[turn, 0] + col_x[turn, 1]) + (col_x[turn, 2] + col_x[turn, 3])
        copies = [
            remote(
                col_z.at[turn, z],
                col_z.at[turn, z],
                colz_send.at[turn * 7 + step - 1],
                colz_recv.at[turn * 7 + step - 1],
                along_z(step),
            )
            for step in range(1, 8)
        ]
        for copy in copies:
            copy.start()
        for copy in copies:
            copy.wait()
        total = col_z[turn, 0]
        for other in range(1, 8):
            total = total + col_z[turn, other]
        result = 1.0 / (CENTROIDS * total)
        for quarter in range(QUARTERS):
            line = jnp.concatenate(
                [result[2 * quarter : 2 * quarter + 1], result[2 * quarter + 1 : 2 * quarter + 2]],
                axis=1,
            )
            scale[quarter] = jnp.broadcast_to(line, (8, COLS))

    def row_sums(turn):
        def body(at, _):
            total = None
            for quarter in range(QUARTERS):
                weights = score[quarter, pl.ds(pl.multiple_of(at * BLOCK, BLOCK), BLOCK), :]
                weights = weights.reshape(BLOCK // 8, 8, COLS) * scale[quarter][None]
                weights = weights.reshape(BLOCK, COLS)
                for part in range(COLS // BLOCK):
                    piece = weights[:, part * BLOCK : (part + 1) * BLOCK]
                    total = piece if total is None else total + piece
            rows[turn, host, pl.ds(at, 1), :] = jnp.sum(total.T, axis=0, keepdims=True)
            return 0

        lax.fori_loop(0, BLOCKS, body, 0)
        copies = [
            remote(
                rows.at[turn, host],
                rows.at[turn, host],
                row_send.at[turn * 7 + step - 1],
                row_recv.at[turn * 7 + step - 1],
                along_host(step),
            )
            for step in range(1, 8)
        ]
        for copy in copies:
            copy.start()
        for copy in copies:
            copy.wait()
        total = rows[turn, 0]
        for other in range(1, HOSTS):
            total = total + rows[turn, other]
        return 1.0 / (DOCS * total)

    exchange_columns(0)

    doc_row[...] = row_sums(0) * live[...]

    def column_body(at, sums):
        line = jnp.broadcast_to(doc_row[pl.ds(at, 1), :], (BLOCK, BLOCK)).T
        line = wide(line)
        out = []
        for quarter in range(QUARTERS):
            weights = score[quarter, pl.ds(pl.multiple_of(at * BLOCK, BLOCK), BLOCK), :] * line
            out.append(sums[quarter] + jnp.sum(weights.reshape(BLOCK // 8, 8, COLS), axis=0))
        return tuple(out)

    sums = lax.fori_loop(
        0, BLOCKS, column_body, tuple(jnp.zeros((8, COLS), F32) for _ in range(QUARTERS))
    )
    for quarter in range(QUARTERS):
        col_acc[quarter] = sums[quarter]
    exchange_columns(1)

    doc_scale = row_sums(1)
    doc_log[hi, 0:BLOCKS, :] = jnp.log(DOCS * doc_scale)
    for which in range(HOSTS):
        doc_log[hi, BLOCKS + which : BLOCKS + which + 1, :] = live_counts[which, 0:1, :]
    log_copies = [
        remote(
            doc_log.at[hi],
            doc_log.at[hi],
            log_send.at[step - 1],
            log_recv.at[step - 1],
            along_z(2 * step),
        )
        for step in range(1, 4)
    ]
    for copy in log_copies:
        copy.start()
    doc_row[...] = DOCS * doc_scale * live[...]

    def spread(at, _):
        line = jnp.broadcast_to(doc_row[pl.ds(at, 1), :], (BLOCK, BLOCK)).T
        doc_col[pl.ds(pl.multiple_of(at * BLOCK, BLOCK), BLOCK), :] = line
        return 0

    lax.fori_loop(0, BLOCKS, spread, 0)

    share = WIDTH // 8
    left_x, right_x, far_x = mod(x + 3, 4), mod(x + 1, 4), mod(x + 2, 4)
    to_up, to_down = along_x(1), along_x(3)

    def piece(owner, half):
        return pl.ds(pl.multiple_of(owner * (2 * share) + half * share, 8), share)

    halves = (pl.ds(0, share), pl.ds(share, share))

    def sum_copies(at):
        n, f, w = numer.at[at], far.at[at], near.at[at]
        plan = [
            (n.at[piece(far_x, 0)], f.at[0], to_down),
            (n.at[piece(far_x, 1)], f.at[1], to_up),
            (n.at[piece(left_x, 1)], w.at[1, halves[1]], to_down),
            (n.at[piece(right_x, 0)], w.at[0, halves[0]], to_up),
            (n.at[piece(left_x, 0)], w.at[1, halves[0]], to_down),
            (n.at[piece(right_x, 1)], w.at[0, halves[1]], to_up),
        ]
        return [
            remote(src, dst, sum_send.at[at * 6 + i], sum_recv.at[at * 6 + i], target)
            for i, (src, dst, target) in enumerate(plan)
        ]

    def quarter_of(at):
        return mod(hi + 1 + at, QUARTERS)

    def numerators(at):
        quarter = quarter_of(at)
        line = scale[quarter][None]

        def body(which, _):
            weights = score[quarter, pl.ds(pl.multiple_of(which * SLOTS, SLOTS), SLOTS), :]
            factor = wide(doc_col[pl.ds(pl.multiple_of(which * SLOTS, SLOTS), SLOTS), :])
            plan = (factor * weights).reshape(SLOTS // 8, 8, COLS) * line
            plan = plan.reshape(SLOTS, COLS).astype(BF16)
            term = jnp.dot(units_t[which], plan, preferred_element_type=F32)

            @pl.when(which == 0)
            def _():
                numer[at] = term

            @pl.when(which > 0)
            def _():
                numer[at] += term

            return 0

        lax.fori_loop(0, HOSTS, body, 0)

    def share_copy(at, half):
        target = quarter_of(at) * 2 + half
        return target, remote(
            reduced.at[at, halves[half]],
            shares.at[z],
            share_send.at[at * 2 + half],
            share_recv.at[z],
            device(x, y, target, core),
        )

    all_sums = [sum_copies(at) for at in range(QUARTERS)]

    def hand_on(at):
        copies = all_sums[at]
        copies[0].wait_recv()
        numer[at, piece(left_x, 0), :] += far[at, 0]
        copies[4].start()
        copies[1].wait_recv()
        numer[at, piece(right_x, 1), :] += far[at, 1]
        copies[5].start()

    def reduce_x(at):
        copies = all_sums[at]
        for i in (2, 3, 4, 5):
            copies[i].wait_recv()
        mine = numer[at, pl.ds(pl.multiple_of(x * (2 * share), 8), 2 * share), :]
        reduced[at] = mine + near[at, 0] + near[at, 1]
        for half in range(2):
            target, copy = share_copy(at, half)

            @pl.when(target != z)
            def _():
                copy.start()

            @pl.when(target == z)
            def _():
                shares[z] = reduced[at, halves[half], :]

    for at in range(QUARTERS):
        numerators(at)
        for i in range(4):
            all_sums[at][i].start()
        if at >= 1:
            hand_on(at - 1)
        if at >= 2:
            reduce_x(at - 2)

    for copy in log_copies:
        copy.wait()
    counts = jnp.concatenate(
        [doc_log[quarter, BLOCKS : BLOCKS + HOSTS, :] for quarter in range(QUARTERS)], axis=0
    )
    values = jnp.concatenate([doc_log[quarter, 0:BLOCKS, :] for quarter in range(QUARTERS)], axis=0)
    lane = lax.broadcasted_iota(jnp.int32, (32, BLOCK), 1)
    line = lax.broadcasted_iota(jnp.int32, (32, BLOCK), 0)
    owner = lane >> 2
    begin = jnp.sum(jnp.where(line < owner, counts, 0.0), axis=0, keepdims=True)
    held = jnp.sum(jnp.where(line == owner, counts, 0.0), axis=0, keepdims=True)
    slot = (lax.broadcasted_iota(jnp.int32, (1, BLOCK), 1) & 3).astype(F32)
    place = jnp.where(slot < held, begin + slot, -1.0)
    goal = jnp.full((1, BLOCK), -1.0, F32)
    for at in range(64):
        goal = jnp.where(place == float(at), dest_ref[0, at].astype(F32), goal)
    chosen = lax.broadcasted_iota(jnp.int32, (64, BLOCK), 0).astype(F32) == goal
    weights_out[...] = jnp.dot(
        jnp.where(chosen, 1.0, 0.0),
        values,
        precision=lax.Precision.HIGHEST,
        preferred_element_type=F32,
    )

    hand_on(3)
    reduce_x(2)
    reduce_x(3)
    for step in range(1, 8):
        other = mod(z + step, 8)
        remote(
            shares.at[other], shares.at[other], share_send.at[0], share_recv.at[other], along_z(1)
        ).wait_recv()
    total = shares[0]
    for other in range(1, 8):
        total = total + shares[other]
    numer_out[...] = total

    for at in range(QUARTERS):
        for copy in all_sums[at]:
            copy.wait_send()
        for half in range(2):
            target, copy = share_copy(at, half)

            @pl.when(target != z)
            def _():
                copy.wait_send()


def on_device(loader_blocks, block_counts, block_dest, centroids):
    dma = pltpu.SemaphoreType.DMA
    share = WIDTH // 8
    vmem = pl.BlockSpec(memory_space=pltpu.VMEM)
    smem = pl.BlockSpec(memory_space=pltpu.SMEM)
    numer, weights = pl.pallas_call(
        kernel,
        out_shape=(
            jax.ShapeDtypeStruct((share, COLS), F32),
            jax.ShapeDtypeStruct((64, BLOCK), F32),
        ),
        in_specs=[vmem, smem, smem, vmem],
        out_specs=(vmem, vmem),
        scratch_shapes=[
            pltpu.VMEM((HOSTS, SLOTS, WIDTH), BF16),
            pltpu.VMEM((HOSTS, WIDTH, SLOTS), BF16),
            pltpu.VMEM((QUARTERS, WIDTH, COLS), BF16),
            pltpu.VMEM((QUARTERS, HOSTS * SLOTS, COLS), F32),
            pltpu.VMEM((HOSTS, 8, BLOCK), F32),
            pltpu.VMEM((BLOCKS, BLOCK), F32),
            pltpu.VMEM((QUARTERS, 8, COLS), F32),
            pltpu.VMEM((2, 4, 8, 256), F32),
            pltpu.VMEM((2, 8, 8, 256), F32),
            pltpu.VMEM((QUARTERS, 8, COLS), F32),
            pltpu.VMEM((2, HOSTS, BLOCKS, BLOCK), F32),
            pltpu.VMEM((BLOCKS, BLOCK), F32),
            pltpu.VMEM((HOSTS * SLOTS, BLOCK), F32),
            pltpu.VMEM((QUARTERS, WIDTH, COLS), F32),
            pltpu.VMEM((QUARTERS, 2, share, COLS), F32),
            pltpu.VMEM((QUARTERS, 2, 2 * share, COLS), F32),
            pltpu.VMEM((QUARTERS, 2 * share, COLS), F32),
            pltpu.VMEM((8, share, COLS), F32),
            pltpu.VMEM((QUARTERS, BLOCKS + HOSTS, BLOCK), F32),
            dma((13,)),
            dma((13,)),
            dma((12,)),
            dma((12,)),
            dma((7,)),
            dma((7,)),
            dma((6,)),
            dma((6,)),
            dma((14,)),
            dma((14,)),
            dma((14,)),
            dma((14,)),
            dma((3,)),
            dma((3,)),
            dma((24,)),
            dma((24,)),
            dma((8,)),
            dma((8,)),
        ],
        compiler_params=pltpu.CompilerParams(
            collective_id=0, has_side_effects=True, vmem_limit_bytes=62 << 20
        ),
        cost_estimate=pl.CostEstimate(
            flops=13_000_000_000, bytes_accessed=2_000_000, transcendentals=8_400_000
        ),
    )(loader_blocks.reshape(SLOTS, WIDTH), block_counts, block_dest, centroids)
    return numer, weights.reshape(64 * BLOCK)


def solution(mesh):
    in_specs = (P("docs", "cent", None, None), P("docs", "cent"), P("docs", None), P(None, "cent"))
    out_specs = (P("docs", "cent"), P("docs"))
    return jax.shard_map(
        on_device, mesh=mesh, in_specs=in_specs, out_specs=out_specs, check_vma=False
    )
```

time: 1410 us -> 143 us (0.10)
  blocking collectives: 1180 us -> 0 us
  Pallas kernels: 0 us -> 139 us
  waiting for transfers between devices: 106 us -> 0 us
  matrix products: 62.6 us -> 0 us
  other arithmetic: 25.8 us -> 0 us
    psum x18 -> x0, blocking collectives: 1160 us -> none  [the longest x16 1120 us: sweep(): row_sum = lax.psum(row_part, 'cent')]
    pallas_call x0 -> x1, Pallas kernels: none -> 139 us  [on_device(): pl.pallas_call(kernel, out_shape=(jax.ShapeDtypeStruct((share, COLS), F32...]
    all_gather x1 -> x0, waiting for transfers between devices: 74.1 us -> none  [on_device(): lax.all_gather(loader_blocks, 'cent', axis=1, tiled=True)]
    dot_general x32 -> x0, matrix products: 62.6 us -> none  [the longest x24 46.6 us: kernel(): jnp.dot(tile, unit_cents, preferred_element_type=jnp.float32)]
    reduce_scatter x1 -> x0, waiting for transfers between devices: 31.2 us -> none  [on_device(): lax.psum_scatter(numer, 'docs', scatter_dimension=0, tiled=True)]
    unnamed x1 -> x0, blocking collectives: 18.9 us -> none
    convert_element_type x3 -> x0, other arithmetic: 18.8 us -> none  [the longest x1 9.23 us: unit_rows(): values = rows.astype(jnp.float32)]
  transfers between devices with their start and end apart: 2 -> 0, of which waited for: 2 -> 0; matrix products, arithmetic and copies ran while one was open for 0% -> 0% of each run, Pallas kernels for 0% -> 0%
where the time goes in v1:
time: 143 us
  Pallas kernels  139 us (97%)
  local copies, waits for them, and re-layouts  2.17 us (2%)
    pallas_call x1, Pallas kernels, on_device(): pl.pallas_call(kernel, out_shape=(jax.ShapeDtypeStruct((share, COLS), F32...  139 us

profile of v1, /device:TPU:1, one launch (start us, length us, event | category | flops | bytes accessed | tf_op | source)
XLA Modules:
  0.0 142.7 jit_solution(465971397119083457)
XLA Ops:
  1.3 139.3 %shard_map.59 = (f32[48,512]{1,0:T(8,128)}, f32[64,128]{1,0:T(8,128)}) custom-call(bf16[512,384]{1,0:T(8,128)(2,1)} %bitcast.3, s32[1,1]{1,0:T(1,128)S(6)} %copy.8.counts_ref, s32[1,64]{1,0:T(1,128)} %dest_ref.1, bf16[384,512]{1,0:T(8,128)(2,1)} %cents_ref.1), custom_call_target="tpu_custom_call" | custom-call | flops 12999999488 | bytes 2000000 | tf_op jit(solution)/shard_map/pallas_call | solution.py:585
  140.6 0.0 copy-start
  140.6 1.5 %copy.9 = f32[48,512]{1,0:T(8,128)} copy(f32[48,512]{1,0:T(8,128)} %get-tuple-element.8) | data formatting | bytes 196608
  142.1 0.0 copy-done
  142.1 0.6 copy.10
Async XLA Ops:
  140.6 1.6 %copy-start = (f32[64,128]{1,0:T(8,128)S(1)}, f32[64,128]{1,0:T(8,128)}, u32[]{:S(2)}) copy-start(f32[64,128]{1,0:T(8,128)} %get-tuple-element.5) | copy-start | bytes 98308

commit v2 on v1

v2 whole, which is shorter than its diff:
```python
import jax
import jax.numpy as jnp
from jax import lax
from jax.experimental import pallas as pl
from jax.experimental.pallas import tpu as pltpu
from jax.sharding import PartitionSpec as P

F32 = jnp.float32
BF16 = jnp.bfloat16

WIDTH = 384
COLS = 512
SLOTS = 512
BLOCK = 128
MOST = 4
HOSTS = 8
BLOCKS = HOSTS * MOST
QUARTERS = 4
SHARPNESS = 25.0
LOG2_E = 1.4426950408889634
STEP = 1.99
DOCS = 65536.0
CENTROIDS = 16384.0


def mod(value, size):
    return lax.rem(value, jnp.int32(size))


def wide(tile):
    return jnp.concatenate([tile] * (COLS // BLOCK), axis=1)


def device(x, y, z, core):
    return (x * 2 + mod(z, 2), (lax.div(z, jnp.int32(2)) * 4 + y) * 2 + core)


def kernel(
    docs_hbm,
    counts_ref,
    dest_ref,
    cents_hbm,
    numer_out,
    weights_out,
    units,
    units_t,
    cents,
    score,
    live_counts,
    live,
    col_acc,
    col_x,
    col_z,
    scale,
    rows,
    doc_row,
    doc_col,
    numer,
    out_x,
    in_x,
    out_z,
    in_z,
    reduced,
    doc_log,
    docs_ref,
    cents_ref,
    load_sem,
    unit_send,
    unit_recv,
    cent_send,
    cent_recv,
    count_send,
    count_recv,
    colx_send,
    colx_recv,
    colz_send,
    colz_recv,
    row_send,
    row_recv,
    log_send,
    log_recv,
    sum_send,
    sum_recv,
    share_send,
    share_recv,
):
    doc_index = lax.axis_index("docs")
    cent_index = lax.axis_index("cent")
    x = lax.div(doc_index, jnp.int32(2))
    lo = mod(doc_index, 2)
    core = mod(cent_index, 2)
    y = mod(lax.div(cent_index, jnp.int32(2)), 4)
    hi = lax.div(cent_index, jnp.int32(8))
    z = hi * 2 + lo
    host = y * 2 + core

    def along_host(step):
        other = mod(host + step, HOSTS)
        return device(x, lax.div(other, jnp.int32(2)), z, mod(other, 2))

    def along_x(step):
        return device(mod(x + step, 4), y, z, core)

    def along_z(step):
        return device(x, y, mod(z + step, 8), core)

    def along_y(step):
        return device(x, mod(y + step, 4), z, core)

    def remote(src, dst, send, recv, target):
        return pltpu.make_async_remote_copy(
            src_ref=src,
            dst_ref=dst,
            send_sem=send,
            recv_sem=recv,
            device_id=target,
            device_id_type=pl.DeviceIdType.MESH,
        )

    to_right, to_left = along_y(1), along_y(3)
    to_twin = device(x, y, z, 1 - core)

    barrier = pltpu.get_barrier_semaphore()
    greeted = [along_z(1), along_z(7)]
    greeted += [along_host(step) for step in range(1, 8)]
    greeted += [along_x(step) for step in range(1, 4)]
    for other in greeted:
        pl.semaphore_signal(
            barrier, inc=1, device_id=other, device_id_type=pl.DeviceIdType.MESH
        )
    load_docs = pltpu.make_async_copy(docs_hbm, docs_ref, load_sem.at[0])
    load_cents = pltpu.make_async_copy(cents_hbm, cents_ref, load_sem.at[1])
    load_docs.start()
    load_cents.start()

    load_docs.wait()
    values = docs_ref[...].astype(F32)
    factor = lax.rsqrt(jnp.mean(values * values, axis=1, keepdims=True) + 1e-06)
    units[host] = (values * factor * WIDTH ** (-0.5)).astype(BF16)
    load_cents.wait()
    values = cents_ref[...].astype(F32)
    factor = lax.rsqrt(jnp.mean(values * values, axis=0, keepdims=True) + 1e-06)
    cents[hi] = (values * factor * WIDTH ** (-0.5)).astype(BF16)
    live_counts[host] = jnp.full((8, BLOCK), counts_ref[0, 0].astype(F32), F32)
    col_acc[...] = jnp.zeros_like(col_acc)

    pl.semaphore_wait(barrier, 12)

    left_y, right_y, far_y = mod(y + 3, 4), mod(y + 1, 4), mod(y + 2, 4)
    first, second, whole = pl.ds(0, SLOTS // 2), pl.ds(SLOTS // 2, SLOTS // 2), pl.ds(0, SLOTS)
    own, from_left, from_right, across = (
        host,
        left_y * 2 + core,
        right_y * 2 + core,
        far_y * 2 + core,
    )
    unit_plan = [
        (own, first, to_right),
        (own, second, to_right),
        (own, first, to_left),
        (own, second, to_left),
        (from_left, first, to_right),
        (from_right, second, to_left),
        (own, whole, to_twin),
        (from_left, first, to_twin),
        (from_left, second, to_twin),
        (from_right, first, to_twin),
        (from_right, second, to_twin),
        (across, first, to_twin),
        (across, second, to_twin),
    ]
    unit_copies = []
    for at, (which, part, target) in enumerate(unit_plan):
        ref = units.at[which, part]
        unit_copies.append(remote(ref, ref, unit_send.at[at], unit_recv.at[at], target))

    chunk = WIDTH // 4
    rising, falling = [], []
    for step in range(6):
        back = 1 if step < 4 else 2
        which = mod(hi - back + lo + 4, QUARTERS)
        ref = cents.at[which, pl.ds((step % 4) * chunk, chunk)]
        rising.append(remote(ref, ref, cent_send.at[step], cent_recv.at[step], along_z(1)))
        ahead = 0 if step < 4 else 1
        which = mod(hi + ahead + lo, QUARTERS)
        ref = cents.at[which, pl.ds(((step + 2) % 4) * chunk, chunk)]
        falling.append(
            remote(ref, ref, cent_send.at[6 + step], cent_recv.at[6 + step], along_z(7))
        )

    def cent_open(steps):
        @pl.when(lo == 1)
        def _():
            for step in steps:
                rising[step].start()

        @pl.when(lo == 0)
        def _():
            for step in steps:
                falling[step].start()

    def cent_start(step):
        @pl.when(lo == 1)
        def _():
            if step >= 4:
                rising[step - 4].wait_recv()
                rising[step].start()
            falling[step].wait_recv()
            falling[step].start()

        @pl.when(lo == 0)
        def _():
            if step >= 4:
                falling[step - 4].wait_recv()
                falling[step].start()
            rising[step].wait_recv()
            rising[step].start()

    def cent_finish(steps):
        @pl.when(lo == 1)
        def _():
            for step in steps:
                rising[step].wait_recv()

        @pl.when(lo == 0)
        def _():
            for step in steps:
                falling[step].wait_recv()

    count_copies = [
        remote(
            live_counts.at[host],
            live_counts.at[host],
            count_send.at[step - 1],
            count_recv.at[step - 1],
            along_host(step),
        )
        for step in range(1, 8)
    ]
    def score_tiles(which, turns):
        for turn in turns:
            quarter = mod(hi + (turn ^ (turn >> 1)), QUARTERS)
            logits = jnp.dot(units[which], cents[quarter], preferred_element_type=F32)
            weights = jnp.exp2((SHARPNESS * LOG2_E) * logits)
            score[quarter, pl.ds(pl.multiple_of(which * SLOTS, SLOTS), SLOTS), :] = weights
            total = col_acc[quarter]
            for slot in range(MOST):
                part = weights[slot * BLOCK : (slot + 1) * BLOCK]
                part = jnp.sum(part.reshape(BLOCK // 8, 8, COLS), axis=0)
                here = jnp.where(live_counts[which] > slot, 1.0, 0.0)
                total = total + part * wide(here)
            col_acc[quarter] = total

    def score_hosts(count, host_of, turns, unroll):
        def body(at, _):
            score_tiles(host_of(at), turns)
            return 0

        lax.fori_loop(0, count, body, 0, unroll=unroll)

    def take(*numbers):
        for at in numbers:
            unit_copies[at].wait_recv()

    def give(*numbers):
        for at in numbers:
            unit_copies[at].start()

    give(0, 3)
    cent_open((0, 1))
    give(6)
    for copy in count_copies:
        copy.start()
    take(6)
    for copy in count_copies:
        copy.wait_recv()
    give(1, 2)
    cent_open((2, 3))
    score_hosts(2, lambda at: y * 2 + (core ^ at), (0,), 2)
    cent_start(0)
    take(0, 3)
    give(4, 5, 7, 10)
    cent_start(1)
    cent_start(2)
    take(1, 2)
    give(8, 9)
    cent_start(3)
    cent_start(4)
    take(7, 8, 9, 10)
    score_hosts(4, lambda at: mod(y + 1 + 2 * (at >> 1), 4) * 2 + (core ^ (at & 1)), (0,), 2)
    cent_start(5)
    cent_finish((2, 3))
    score_hosts(6, lambda at: mod(y + 3 + (at >> 1), 4) * 2 + (core ^ (at & 1)), (1, 2), 2)
    take(4, 5)
    give(11, 12)
    cent_finish((4, 5))
    score_hosts(6, lambda at: mod(y + 3 + (at >> 1), 4) * 2 + (core ^ (at & 1)), (3,), 3)
    take(11, 12)
    score_hosts(2, lambda at: far_y * 2 + (core ^ at), (0, 1, 2, 3), 2)

    for at in range(13):
        unit_copies[at].wait_send()
    for step in range(6):
        rising[step].wait_send()
        falling[step].wait_send()
    for copy in count_copies:
        copy.wait_send()

    for which in range(HOSTS):
        units_t[which] = units[which].T
        for slot in range(MOST):
            at = which * MOST + slot
            live[at : at + 1, :] = jnp.where(live_counts[which, 0:1, :] > slot, 1.0, 0.0)

    def exchange_columns(turn):
        for quarter in range(QUARTERS):
            total = jnp.sum(col_acc[quarter], axis=0, keepdims=True)
            for part in range(2):
                col_x[turn, x, 2 * quarter + part : 2 * quarter + part + 1, :] = total[
                    :, part * 256 : (part + 1) * 256
                ]
        copies = [
            remote(
                col_x.at[turn, x],
                col_x.at[turn, x],
                colx_send.at[turn * 3 + step - 1],
                colx_recv.at[turn * 3 + step - 1],
                along_x(step),
            )
            for step in range(1, 4)
        ]
        for copy in copies:
            copy.start()
        for copy in copies:
            copy.wait()
        col_z[turn, z] = (col_x[turn, 0] + col_x[turn, 1]) + (col_x[turn, 2] + col_x[turn, 3])
        copies = [
            remote(
                col_z.at[turn, z],
                col_z.at[turn, z],
                colz_send.at[turn * 7 + step - 1],
                colz_recv.at[turn * 7 + step - 1],
                along_z(step),
            )
            for step in range(1, 8)
        ]
        for copy in copies:
            copy.start()
        for copy in copies:
            copy.wait()
        total = col_z[turn, 0]
        for other in range(1, 8):
            total = total + col_z[turn, other]
        result = 1.0 / (CENTROIDS * total)
        for quarter in range(QUARTERS):
            line = jnp.concatenate(
                [result[2 * quarter : 2 * quarter + 1], result[2 * quarter + 1 : 2 * quarter + 2]],
                axis=1,
            )
            scale[quarter] = jnp.broadcast_to(line, (8, COLS))

    half_blocks = BLOCKS // 2

    def row_pass(turn, half):
        def body(at, _):
            total = None
            for quarter in range(QUARTERS):
                weights = score[quarter, pl.ds(pl.multiple_of(at * BLOCK, BLOCK), BLOCK), :]
                weights = weights.reshape(BLOCK // 8, 8, COLS) * scale[quarter][None]
                weights = weights.reshape(BLOCK, COLS)
                for part in range(COLS // BLOCK):
                    piece = weights[:, part * BLOCK : (part + 1) * BLOCK]
                    total = piece if total is None else total + piece
            rows[turn, host, pl.ds(at, 1), :] = jnp.sum(total.T, axis=0, keepdims=True)
            return 0

        lax.fori_loop(half * half_blocks, (half + 1) * half_blocks, body, 0, unroll=4)
        ref = rows.at[turn, host, pl.ds(half * half_blocks, half_blocks)]
        copies = []
        for step in range(1, 8):
            at = (turn * 2 + half) * 7 + step - 1
            copies.append(remote(ref, ref, row_send.at[at], row_recv.at[at], along_host(step)))
        for copy in copies:
            copy.start()
        return copies

    def doc_scales(turn, half, copies):
        for copy in copies:
            copy.wait()
        part = slice(half * half_blocks, (half + 1) * half_blocks)
        total = rows[turn, 0, part, :]
        for other in range(1, HOSTS):
            total = total + rows[turn, other, part, :]
        return part, 1.0 / (DOCS * total)

    exchange_columns(0)

    col_acc[...] = jnp.zeros_like(col_acc)

    def column_body(at, _):
        line = wide(jnp.broadcast_to(doc_row[pl.ds(at, 1), :], (BLOCK, BLOCK)).T)
        for quarter in range(QUARTERS):
            weights = score[quarter, pl.ds(pl.multiple_of(at * BLOCK, BLOCK), BLOCK), :] * line
            col_acc[quarter] += jnp.sum(weights.reshape(BLOCK // 8, 8, COLS), axis=0)
        return 0

    sent = [row_pass(0, half) for half in range(2)]
    for half in range(2):
        part, doc_scale = doc_scales(0, half, sent[half])
        doc_row[part, :] = doc_scale * live[part, :]
        lax.fori_loop(half * half_blocks, (half + 1) * half_blocks, column_body, 0, unroll=4)
    exchange_columns(1)

    def spread(at, _):
        line = jnp.broadcast_to(doc_row[pl.ds(at, 1), :], (BLOCK, BLOCK)).T
        doc_col[pl.ds(pl.multiple_of(at * BLOCK, BLOCK), BLOCK), :] = line
        return 0

    share = WIDTH // 8
    tall = 2 * share

    def encode(values, ref):
        most = jnp.max(jnp.abs(values), axis=0, keepdims=True)
        power = jnp.ceil(jnp.log2(jnp.maximum(most, 1e-30)))
        steps = jnp.round(values * (jnp.exp2(14.0 - power) * STEP))
        count = values.shape[0]
        ref[0:count, :] = steps.astype(jnp.int32).astype(jnp.int16)
        ref[count : count + 16, :] = (
            jnp.broadcast_to(power, (16, COLS)).astype(jnp.int32).astype(jnp.int16)
        )

    def decode(ref, count):
        power = ref[count : count + 16, :].astype(jnp.int32).astype(F32)[0:1]
        steps = ref[0:count, :].astype(jnp.int32).astype(F32)
        return steps * (jnp.exp2(power - 14.0) * (1.0 / STEP))

    def rows_of(owner):
        return pl.ds(pl.multiple_of(owner * tall, 8), tall)

    def sum_copies(at):
        return [
            remote(
                out_x.at[at, step - 1],
                in_x.at[at, step - 1],
                sum_send.at[at * 3 + step - 1],
                sum_recv.at[at * 3 + step - 1],
                along_x(step),
            )
            for step in range(1, 4)
        ]

    def quarter_of(at):
        return mod(hi + 1 + at, QUARTERS)

    def numerators(at, half):
        quarter = quarter_of(at)
        line = scale[quarter][None]
        total = None
        for which in range(half * HOSTS // 2, (half + 1) * HOSTS // 2):
            here = slice(which * SLOTS, (which + 1) * SLOTS)
            factor = wide(doc_col[here, :])
            plan = (factor * score[quarter, here, :]).reshape(SLOTS // 8, 8, COLS) * line
            plan = plan.reshape(SLOTS, COLS).astype(BF16)
            term = jnp.dot(units_t[which], plan, preferred_element_type=F32)
            total = term if total is None else total + term
        if half == 0:
            numer[at] = total
        else:
            numer[at] += total

    def share_copy(at, half):
        return remote(
            out_z.at[at, half],
            in_z.at[z],
            share_send.at[at * 2 + half],
            share_recv.at[z],
            device(x, y, quarter_of(at) * 2 + half, core),
        )

    last = QUARTERS - 1
    other_half = pl.ds(pl.multiple_of((1 - lo) * share, 8), share)
    own_half = pl.ds(pl.multiple_of(lo * share, 8), share)
    all_sums = [sum_copies(at) for at in range(QUARTERS)]
    all_shares = [share_copy(at, half) for at in range(last) for half in range(2)]
    all_shares.append(
        remote(
            out_z.at[last, 0],
            in_z.at[z],
            share_send.at[last * 2],
            share_recv.at[z],
            device(x, y, hi * 2 + 1 - lo, core),
        )
    )

    def send_x(at):
        for step in (2, 1, 3):
            encode(numer[at, rows_of(mod(x + step, 4)), :], out_x.at[at, step - 1])
            all_sums[at][step - 1].start()

    def reduce_x(at):
        total = numer[at, rows_of(x), :]
        for step in (1, 3, 2):
            all_sums[at][step - 1].wait_recv()
            total = total + decode(in_x.at[at, step - 1], tall)
        if at < last:
            for half in range(2):
                encode(total[half * share : (half + 1) * share], out_z.at[at, half])
                all_shares[at * 2 + half].start()
        else:
            reduced[...] = total
            encode(reduced[other_half, :], out_z.at[last, 0])
            all_shares[-1].start()

    sent = [row_pass(1, half) for half in range(2)]
    for half in range(2):
        part, doc_scale = doc_scales(1, half, sent[half])
        doc_log[hi, part, :] = jnp.log(DOCS * doc_scale)
        doc_row[part, :] = DOCS * doc_scale * live[part, :]
        lax.fori_loop(half * half_blocks, (half + 1) * half_blocks, spread, 0, unroll=4)
        numerators(0, half)
    for which in range(HOSTS):
        doc_log[hi, BLOCKS + which : BLOCKS + which + 1, :] = live_counts[which, 0:1, :]
    log_copies = [
        remote(
            doc_log.at[hi],
            doc_log.at[hi],
            log_send.at[step - 1],
            log_recv.at[step - 1],
            along_z(2 * step),
        )
        for step in range(1, 4)
    ]
    for copy in log_copies:
        copy.start()

    for at in range(QUARTERS):
        if at > 0:
            numerators(at, 0)
            numerators(at, 1)
        send_x(at)
        if at >= 2:
            reduce_x(at - 2)

    for copy in log_copies:
        copy.wait()
    counts = jnp.concatenate(
        [doc_log[quarter, BLOCKS : BLOCKS + HOSTS, :] for quarter in range(QUARTERS)], axis=0
    )
    values = jnp.concatenate([doc_log[quarter, 0:BLOCKS, :] for quarter in range(QUARTERS)], axis=0)
    lane = lax.broadcasted_iota(jnp.int32, (32, BLOCK), 1)
    line = lax.broadcasted_iota(jnp.int32, (32, BLOCK), 0)
    owner = lane >> 2
    begin = jnp.sum(jnp.where(line < owner, counts, 0.0), axis=0, keepdims=True)
    held = jnp.sum(jnp.where(line == owner, counts, 0.0), axis=0, keepdims=True)
    slot = (lax.broadcasted_iota(jnp.int32, (1, BLOCK), 1) & 3).astype(F32)
    place = jnp.where(slot < held, begin + slot, -1.0)
    goal = jnp.full((1, BLOCK), -1.0, F32)
    for at in range(64):
        goal = jnp.where(place == float(at), dest_ref[0, at].astype(F32), goal)
    chosen = lax.broadcasted_iota(jnp.int32, (64, BLOCK), 0).astype(F32) == goal
    weights_out[...] = jnp.dot(
        jnp.where(chosen, 1.0, 0.0),
        values,
        precision=lax.Precision.HIGHEST,
        preferred_element_type=F32,
    )

    reduce_x(2)
    reduce_x(3)
    total = reduced[own_half, :]
    for step in range(1, 8):
        other = mod(z + step, 8)
        remote(
            in_z.at[other], in_z.at[other], share_send.at[0], share_recv.at[other], along_z(1)
        ).wait_recv()
        total = total + decode(in_z.at[other], share)
    numer_out[...] = total

    for at in range(QUARTERS):
        for copy in all_sums[at]:
            copy.wait_send()
    for copy in all_shares:
        copy.wait_send()


def on_device(loader_blocks, block_counts, block_dest, centroids):
    dma = pltpu.SemaphoreType.DMA
    share = WIDTH // 8
    vmem = pl.BlockSpec(memory_space=pltpu.VMEM)
    smem = pl.BlockSpec(memory_space=pltpu.SMEM)
    anywhere = pl.BlockSpec(memory_space=pl.ANY)
    numer, weights = pl.pallas_call(
        kernel,
        out_shape=(
            jax.ShapeDtypeStruct((share, COLS), F32),
            jax.ShapeDtypeStruct((64, BLOCK), F32),
        ),
        in_specs=[anywhere, smem, smem, anywhere],
        out_specs=(vmem, vmem),
        scratch_shapes=[
            pltpu.VMEM((HOSTS, SLOTS, WIDTH), BF16),
            pltpu.VMEM((HOSTS, WIDTH, SLOTS), BF16),
            pltpu.VMEM((QUARTERS, WIDTH, COLS), BF16),
            pltpu.VMEM((QUARTERS, HOSTS * SLOTS, COLS), F32),
            pltpu.VMEM((HOSTS, 8, BLOCK), F32),
            pltpu.VMEM((BLOCKS, BLOCK), F32),
            pltpu.VMEM((QUARTERS, 8, COLS), F32),
            pltpu.VMEM((2, 4, 8, 256), F32),
            pltpu.VMEM((2, 8, 8, 256), F32),
            pltpu.VMEM((QUARTERS, 8, COLS), F32),
            pltpu.VMEM((2, HOSTS, BLOCKS, BLOCK), F32),
            pltpu.VMEM((BLOCKS, BLOCK), F32),
            pltpu.VMEM((HOSTS * SLOTS, BLOCK), F32),
            pltpu.VMEM((QUARTERS, WIDTH, COLS), F32),
            pltpu.VMEM((QUARTERS, 3, 2 * share + 16, COLS), jnp.int16),
            pltpu.VMEM((QUARTERS, 3, 2 * share + 16, COLS), jnp.int16),
            pltpu.VMEM((QUARTERS, 2, share + 16, COLS), jnp.int16),
            pltpu.VMEM((8, share + 16, COLS), jnp.int16),
            pltpu.VMEM((2 * share, COLS), F32),
            pltpu.VMEM((QUARTERS, BLOCKS + HOSTS, BLOCK), F32),
            pltpu.VMEM((SLOTS, WIDTH), BF16),
            pltpu.VMEM((WIDTH, COLS), BF16),
            dma((2,)),
            dma((13,)),
            dma((13,)),
            dma((12,)),
            dma((12,)),
            dma((7,)),
            dma((7,)),
            dma((6,)),
            dma((6,)),
            dma((14,)),
            dma((14,)),
            dma((28,)),
            dma((28,)),
            dma((3,)),
            dma((3,)),
            dma((12,)),
            dma((12,)),
            dma((8,)),
            dma((8,)),
        ],
        compiler_params=pltpu.CompilerParams(
            collective_id=0, has_side_effects=True, vmem_limit_bytes=62 << 20
        ),
        cost_estimate=pl.CostEstimate(
            flops=13_000_000_000, bytes_accessed=2_000_000, transcendentals=8_400_000
        ),
    )(loader_blocks.reshape(SLOTS, WIDTH), block_counts, block_dest, centroids)
    return numer, weights.reshape(64 * BLOCK)


def solution(mesh):
    in_specs = (P("docs", "cent", None, None), P("docs", "cent"), P("docs", None), P(None, "cent"))
    out_specs = (P("docs", "cent"), P("docs"))
    return jax.shard_map(
        on_device, mesh=mesh, in_specs=in_specs, out_specs=out_specs, check_vma=False
    )
```

time: 143 us -> 108 us (0.76)
  Pallas kernels: 139 us -> 104 us
    pallas_call x1, Pallas kernels: 139 us -> 104 us  [on_device(): pl.pallas_call(kernel, out_shape=(jax.ShapeDtypeStruct((share, COLS), F32...]
where the time goes in v2:
time: 108 us
  Pallas kernels  104 us (96%)
  local copies, waits for them, and re-layouts  2.17 us (2%)
  between operations  1.29 us (1%)
    pallas_call x1, Pallas kernels, on_device(): pl.pallas_call(kernel, out_shape=(jax.ShapeDtypeStruct((share, COLS), F32...  104 us
    unnamed x4, local copies, waits for them, and re-layouts  2.17 us

profile of v2, /device:TPU:1, one launch (start us, length us, event | category | flops | bytes accessed | tf_op | source)
XLA Modules:
  0.0 107.7 jit_solution(16352462597598295684)
XLA Ops:
  1.3 104.3 %shard_map.59 = (f32[48,512]{1,0:T(8,128)}, f32[64,128]{1,0:T(8,128)}) custom-call(bf16[512,384]{1,0:T(8,128)(2,1)} %bitcast.3, s32[1,1]{1,0:T(1,128)S(6)} %copy.8.counts_ref, s32[1,64]{1,0:T(1,128)} %dest_ref.1, bf16[384,512]{1,0:T(8,128)(2,1)} %cents_hbm.1), custom_call_target="tpu_custom_call" | custom-call | flops 12999999488 | bytes 2000000 | tf_op jit(solution)/shard_map/pallas_call | solution.py:592
  105.5 0.0 copy-start
  105.6 1.5 %copy.9 = f32[48,512]{1,0:T(8,128)} copy(f32[48,512]{1,0:T(8,128)} %get-tuple-element.8) | data formatting | bytes 196608
  107.1 0.0 copy-done
  107.1 0.6 copy.10
Async XLA Ops:
  105.5 1.6 %copy-start = (f32[64,128]{1,0:T(8,128)S(1)}, f32[64,128]{1,0:T(8,128)}, u32[]{:S(2)}) copy-start(f32[64,128]{1,0:T(8,128)} %get-tuple-element.5) | copy-start | bytes 98308

commit v3 on v2

--- a/solution.py
+++ b/solution.py
@@ -43,7 +43,6 @@
     numer_out,
     weights_out,
     units,
-    units_t,
     cents,
     score,
     live_counts,
@@ -56,8 +55,10 @@
     doc_row,
     doc_col,
     numer,
-    out_x,
-    in_x,
+    open_out,
+    open_in,
+    close_out,
+    close_in,
     out_z,
     in_z,
     reduced,
@@ -144,7 +145,18 @@
     live_counts[host] = jnp.full((8, BLOCK), counts_ref[0, 0].astype(F32), F32)
     col_acc[...] = jnp.zeros_like(col_acc)
 
-    pl.semaphore_wait(barrier, 12)
+    def score_tiles(which, quarters):
+        for quarter in quarters:
+            logits = jnp.dot(units[which], cents[quarter], preferred_element_type=F32)
+            weights = jnp.exp2((SHARPNESS * LOG2_E) * logits)
+            score[quarter, pl.ds(pl.multiple_of(which * SLOTS, SLOTS), SLOTS), :] = weights
+            total = col_acc[quarter]
+            for slot in range(MOST):
+                part = weights[slot * BLOCK : (slot + 1) * BLOCK]
+                part = jnp.sum(part.reshape(BLOCK // 8, 8, COLS), axis=0)
+                here = jnp.where(live_counts[which] > slot, 1.0, 0.0)
+                total = total + part * wide(here)
+            col_acc[quarter] = total
 
     left_y, right_y, far_y = mod(y + 3, 4), mod(y + 1, 4), mod(y + 2, 4)
     first, second, whole = pl.ds(0, SLOTS // 2), pl.ds(SLOTS // 2, SLOTS // 2), pl.ds(0, SLOTS)
@@ -174,58 +186,22 @@
         ref = units.at[which, part]
         unit_copies.append(remote(ref, ref, unit_send.at[at], unit_recv.at[at], target))
 
-    chunk = WIDTH // 4
-    rising, falling = [], []
-    for step in range(6):
-        back = 1 if step < 4 else 2
-        which = mod(hi - back + lo + 4, QUARTERS)
-        ref = cents.at[which, pl.ds((step % 4) * chunk, chunk)]
-        rising.append(remote(ref, ref, cent_send.at[step], cent_recv.at[step], along_z(1)))
-        ahead = 0 if step < 4 else 1
-        which = mod(hi + ahead + lo, QUARTERS)
-        ref = cents.at[which, pl.ds(((step + 2) % 4) * chunk, chunk)]
-        falling.append(
-            remote(ref, ref, cent_send.at[6 + step], cent_recv.at[6 + step], along_z(7))
-        )
-
-    def cent_open(steps):
-        @pl.when(lo == 1)
-        def _():
-            for step in steps:
-                rising[step].start()
-
-        @pl.when(lo == 0)
-        def _():
-            for step in steps:
-                falling[step].start()
-
-    def cent_start(step):
-        @pl.when(lo == 1)
-        def _():
-            if step >= 4:
-                rising[step - 4].wait_recv()
-                rising[step].start()
-            falling[step].wait_recv()
-            falling[step].start()
-
-        @pl.when(lo == 0)
-        def _():
-            if step >= 4:
-                falling[step - 4].wait_recv()
-                falling[step].start()
-            rising[step].wait_recv()
-            rising[step].start()
-
-    def cent_finish(steps):
-        @pl.when(lo == 1)
-        def _():
-            for step in steps:
-                rising[step].wait_recv()
-
-        @pl.when(lo == 0)
-        def _():
-            for step in steps:
-                falling[step].wait_recv()
+    chunk = WIDTH // 8
+    relay_way, origin_way = lo, 1 - lo
+    relay_to, origin_to = along_z(1 + 6 * lo), along_z(7 - 6 * lo)
+    relay_quarter = mod(hi + 3 + 2 * lo, QUARTERS)
+    other_quarter = mod(hi + 5 - 2 * lo, QUARTERS)
+    far_quarter = mod(hi + 2, QUARTERS)
+    relays, origins = [], []
+    for step in range(12):
+        for copies, way, target, blocks in (
+            (relays, relay_way, relay_to, (relay_quarter, far_quarter)),
+            (origins, origin_way, origin_to, (hi, other_quarter)),
+        ):
+            line = mod(step + 4 * way, 8) * chunk
+            ref = cents.at[blocks[step // 8], pl.ds(pl.multiple_of(line, 16), chunk)]
+            at = way * 12 + step
+            copies.append(remote(ref, ref, cent_send.at[at], cent_recv.at[at], target))
 
     count_copies = [
         remote(
@@ -237,26 +213,6 @@
         )
         for step in range(1, 8)
     ]
-    def score_tiles(which, turns):
-        for turn in turns:
-            quarter = mod(hi + (turn ^ (turn >> 1)), QUARTERS)
-            logits = jnp.dot(units[which], cents[quarter], preferred_element_type=F32)
-            weights = jnp.exp2((SHARPNESS * LOG2_E) * logits)
-            score[quarter, pl.ds(pl.multiple_of(which * SLOTS, SLOTS), SLOTS), :] = weights
-            total = col_acc[quarter]
-            for slot in range(MOST):
-                part = weights[slot * BLOCK : (slot + 1) * BLOCK]
-                part = jnp.sum(part.reshape(BLOCK // 8, 8, COLS), axis=0)
-                here = jnp.where(live_counts[which] > slot, 1.0, 0.0)
-                total = total + part * wide(here)
-            col_acc[quarter] = total
-
-    def score_hosts(count, host_of, turns, unroll):
-        def body(at, _):
-            score_tiles(host_of(at), turns)
-            return 0
-
-        lax.fori_loop(0, count, body, 0, unroll=unroll)
 
     def take(*numbers):
         for at in numbers:
@@ -266,48 +222,91 @@
         for at in numbers:
             unit_copies[at].start()
 
-    give(0, 3)
-    cent_open((0, 1))
-    give(6)
+    def relay(*steps):
+        for step in steps:
+            relays[step].wait_recv()
+            relays[step].start()
+
+    def onward(*steps):
+        for step in steps:
+            origins[step].wait_recv()
+            origins[step + 8].start()
+
+    def score_hosts(count, host_of, quarters, unroll):
+        def body(at, _):
+            score_tiles(host_of(at), quarters)
+            return 0
+
+        lax.fori_loop(0, count, body, 0, unroll=unroll)
+
+    def here(at):
+        return y * 2 + (core ^ at)
+
+    def sides(at):
+        return mod(y + 1 + 2 * at, 4) * 2 + core
+
+    def sides_twin(at):
+        return mod(y + 1 + 2 * at, 4) * 2 + 1 - core
+
+    def near(at):
+        return mod(y + 3 + (at >> 1), 4) * 2 + (core ^ (at & 1))
+
+    score_tiles(host, (hi,))
+    pl.semaphore_wait(barrier, 12)
+
     for copy in count_copies:
         copy.start()
-    take(6)
+    give(0, 3, 6)
+    for step in range(8):
+        origins[step].start()
+    give(1, 2)
+    relay(0)
     for copy in count_copies:
         copy.wait_recv()
-    give(1, 2)
-    cent_open((2, 3))
-    score_hosts(2, lambda at: y * 2 + (core ^ at), (0,), 2)
-    cent_start(0)
+    take(6)
+    score_tiles(host ^ 1, (hi,))
+    relay(1, 2, 3)
     take(0, 3)
     give(4, 5, 7, 10)
-    cent_start(1)
-    cent_start(2)
+    relay(4, 5)
+    onward(0)
+    relay(6)
+    onward(1)
+    relay(7)
+    onward(2)
     take(1, 2)
     give(8, 9)
-    cent_start(3)
-    cent_start(4)
+    onward(3)
+    score_hosts(2, here, (relay_quarter,), 2)
+    relay(8)
+    score_hosts(2, sides, (hi, relay_quarter), 2)
+    relay(9)
     take(7, 8, 9, 10)
-    score_hosts(4, lambda at: mod(y + 1 + 2 * (at >> 1), 4) * 2 + (core ^ (at & 1)), (0,), 2)
-    cent_start(5)
-    cent_finish((2, 3))
-    score_hosts(6, lambda at: mod(y + 3 + (at >> 1), 4) * 2 + (core ^ (at & 1)), (1, 2), 2)
+    relay(10)
+    score_hosts(2, sides_twin, (hi, relay_quarter), 2)
+    relay(11)
     take(4, 5)
     give(11, 12)
-    cent_finish((4, 5))
-    score_hosts(6, lambda at: mod(y + 3 + (at >> 1), 4) * 2 + (core ^ (at & 1)), (3,), 3)
+    for step in range(4, 8):
+        origins[step].wait_recv()
+    score_hosts(6, near, (other_quarter,), 3)
+    score_tiles(across, (hi, relay_quarter, other_quarter))
+    for step in range(8, 12):
+        origins[step].wait_recv()
+    score_hosts(6, near, (far_quarter,), 3)
     take(11, 12)
-    score_hosts(2, lambda at: far_y * 2 + (core ^ at), (0, 1, 2, 3), 2)
+    score_tiles(across, (far_quarter,))
+    score_tiles(across ^ 1, (hi, relay_quarter, other_quarter, far_quarter))
 
     for at in range(13):
         unit_copies[at].wait_send()
-    for step in range(6):
-        rising[step].wait_send()
-        falling[step].wait_send()
+    for step in range(12):
+        relays[step].wait_send()
+        origins[step].wait_send()
     for copy in count_copies:
         copy.wait_send()
 
     for which in range(HOSTS):
-        units_t[which] = units[which].T
         for slot in range(MOST):
             at = which * MOST + slot
             live[at : at + 1, :] = jnp.where(live_counts[which, 0:1, :] > slot, 1.0, 0.0)
@@ -418,39 +417,68 @@
 
     share = WIDTH // 8
     tall = 2 * share
-
-    def encode(values, ref):
-        most = jnp.max(jnp.abs(values), axis=0, keepdims=True)
-        power = jnp.ceil(jnp.log2(jnp.maximum(most, 1e-30)))
-        steps = jnp.round(values * (jnp.exp2(14.0 - power) * STEP))
-        count = values.shape[0]
-        ref[0:count, :] = steps.astype(jnp.int32).astype(jnp.int16)
-        ref[count : count + 16, :] = (
-            jnp.broadcast_to(power, (16, COLS)).astype(jnp.int32).astype(jnp.int16)
-        )
-
-    def decode(ref, count):
-        power = ref[count : count + 16, :].astype(jnp.int32).astype(F32)[0:1]
-        steps = ref[0:count, :].astype(jnp.int32).astype(F32)
-        return steps * (jnp.exp2(power - 14.0) * (1.0 / STEP))
-
-    def rows_of(owner):
-        return pl.ds(pl.multiple_of(owner * tall, 8), tall)
+    groups = COLS // BLOCK
+
+    def encode(pieces, ref):
+        row = lax.broadcasted_iota(jnp.int32, (16, BLOCK), 0)
+        powers = jnp.zeros((16, BLOCK), F32)
+        for at, values in enumerate(pieces):
+            most = jnp.max(jnp.abs(values), axis=0, keepdims=True)
+            power = jnp.ceil(jnp.log2(jnp.maximum(most, 1e-30)))
+            steps = jnp.round(values * (jnp.exp2(14.0 - power) * STEP))
+            steps = steps.astype(jnp.int32).astype(jnp.int16)
+            for group in range(groups):
+                place = at * groups + group
+                lanes = slice(group * BLOCK, (group + 1) * BLOCK)
+                ref[place * share : (place + 1) * share, :] = steps[:, lanes]
+                powers = jnp.where(row == place, power[:, lanes], powers)
+        end = len(pieces) * groups * share
+        ref[end : end + 16, :] = powers.astype(jnp.int32).astype(jnp.int16)
+
+    def decode(ref, at, count):
+        end = count * groups * share
+        powers = ref[end : end + 16, :].astype(jnp.int32).astype(F32)
+        factors = jnp.exp2(powers - 14.0) * (1.0 / STEP)
+        out = []
+        for group in range(groups):
+            place = at * groups + group
+            steps = ref[place * share : (place + 1) * share, :].astype(jnp.int32).astype(F32)
+            out.append(steps * factors[place : place + 1])
+        return jnp.concatenate(out, axis=1)
+
+    left_x, right_x, far_x = mod(x + 3, 4), mod(x + 1, 4), mod(x + 2, 4)
+
+    def piece(at, owner, half):
+        return numer[at, pl.ds(pl.multiple_of(owner * tall + half * share, 8), share), :]
+
+    ways = ((1, right_x, 1), (3, left_x, 0))
 
     def sum_copies(at):
-        return [
-            remote(
-                out_x.at[at, step - 1],
-                in_x.at[at, step - 1],
-                sum_send.at[at * 3 + step - 1],
-                sum_recv.at[at * 3 + step - 1],
-                along_x(step),
+        opening, closing = [], []
+        for way, (step, _, _) in enumerate(ways):
+            place = at * 4 + way * 2
+            opening.append(
+                remote(
+                    open_out.at[at, way],
+                    open_in.at[at, way],
+                    sum_send.at[place],
+                    sum_recv.at[place],
+                    along_x(step),
+                )
             )
-            for step in range(1, 4)
-        ]
+            closing.append(
+                remote(
+                    close_out.at[at, way],
+                    close_in.at[at, way],
+                    sum_send.at[place + 1],
+                    sum_recv.at[place + 1],
+                    along_x(step),
+                )
+            )
+        return opening, closing
 
     def quarter_of(at):
-        return mod(hi + 1 + at, QUARTERS)
+        return mod(hi + (2, 1, 3, 0)[at], QUARTERS)
 
     def numerators(at, half):
         quarter = quarter_of(at)
@@ -461,7 +489,9 @@
             factor = wide(doc_col[here, :])
             plan = (factor * score[quarter, here, :]).reshape(SLOTS // 8, 8, COLS) * line
             plan = plan.reshape(SLOTS, COLS).astype(BF16)
-            term = jnp.dot(units_t[which], plan, preferred_element_type=F32)
+            term = lax.dot_general(
+                units[which], plan, (((0,), (0,)), ((), ())), preferred_element_type=F32
+            )
             total = term if total is None else total + term
         if half == 0:
             numer[at] = total
@@ -492,23 +522,30 @@
         )
     )
 
-    def send_x(at):
-        for step in (2, 1, 3):
-            encode(numer[at, rows_of(mod(x + step, 4)), :], out_x.at[at, step - 1])
-            all_sums[at][step - 1].start()
+    def open_x(at):
+        for way, (_, owner, half) in enumerate(ways):
+            encode([piece(at, far_x, half), piece(at, owner, 1 - half)], open_out.at[at, way])
+            all_sums[at][0][way].start()
+
+    def close_x(at):
+        for way, (_, owner, half) in enumerate(ways):
+            all_sums[at][0][way].wait_recv()
+            total = piece(at, owner, half) + decode(open_in.at[at, way], 0, 2)
+            encode([total], close_out.at[at, way])
+            all_sums[at][1][way].start()
 
     def reduce_x(at):
-        total = numer[at, rows_of(x), :]
-        for step in (1, 3, 2):
-            all_sums[at][step - 1].wait_recv()
-            total = total + decode(in_x.at[at, step - 1], tall)
-        if at < last:
-            for half in range(2):
-                encode(total[half * share : (half + 1) * share], out_z.at[at, half])
+        for way, (_, _, half) in enumerate(ways):
+            all_sums[at][1][way].wait_recv()
+            total = piece(at, x, half) + decode(open_in.at[at, 1 - way], 1, 2)
+            total = total + decode(close_in.at[at, way], 0, 1)
+            if at < last:
+                encode([total], out_z.at[at, half])
                 all_shares[at * 2 + half].start()
-        else:
-            reduced[...] = total
-            encode(reduced[other_half, :], out_z.at[last, 0])
+            else:
+                reduced[half * share : (half + 1) * share, :] = total
+        if at == last:
+            encode([reduced[other_half, :]], out_z.at[last, 0])
             all_shares[-1].start()
 
     sent = [row_pass(1, half) for half in range(2)]
@@ -537,9 +574,12 @@
         if at > 0:
             numerators(at, 0)
             numerators(at, 1)
-        send_x(at)
         if at >= 2:
-            reduce_x(at - 2)
+            close_x(at - 2)
+        open_x(at)
+    close_x(2)
+    reduce_x(0)
+    reduce_x(1)
 
     for copy in log_copies:
         copy.wait()
@@ -565,6 +605,7 @@
         preferred_element_type=F32,
     )
 
+    close_x(3)
     reduce_x(2)
     reduce_x(3)
     total = reduced[own_half, :]
@@ -573,11 +614,11 @@
         remote(
             in_z.at[other], in_z.at[other], share_send.at[0], share_recv.at[other], along_z(1)
         ).wait_recv()
-        total = total + decode(in_z.at[other], share)
+        total = total + decode(in_z.at[other], 0, 1)
     numer_out[...] = total
 
     for at in range(QUARTERS):
-        for copy in all_sums[at]:
+        for copy in all_sums[at][0] + all_sums[at][1]:
             copy.wait_send()
     for copy in all_shares:
         copy.wait_send()
@@ -586,20 +627,21 @@
 def on_device(loader_blocks, block_counts, block_dest, centroids):
     dma = pltpu.SemaphoreType.DMA
     share = WIDTH // 8
+    single = share * (COLS // BLOCK) + 16
+    double = 2 * share * (COLS // BLOCK) + 16
     vmem = pl.BlockSpec(memory_space=pltpu.VMEM)
     smem = pl.BlockSpec(memory_space=pltpu.SMEM)
     anywhere = pl.BlockSpec(memory_space=pl.ANY)
     numer, weights = pl.pallas_call(
         kernel,
         out_shape=(
-            jax.ShapeDtypeStruct((share, COLS), F32),
-            jax.ShapeDtypeStruct((64, BLOCK), F32),
+            pltpu.VMEM((share, COLS), F32),
+            pltpu.VMEM((64, BLOCK), F32),
         ),
         in_specs=[anywhere, smem, smem, anywhere],
         out_specs=(vmem, vmem),
         scratch_shapes=[
             pltpu.VMEM((HOSTS, SLOTS, WIDTH), BF16),
-            pltpu.VMEM((HOSTS, WIDTH, SLOTS), BF16),
             pltpu.VMEM((QUARTERS, WIDTH, COLS), BF16),
             pltpu.VMEM((QUARTERS, HOSTS * SLOTS, COLS), F32),
             pltpu.VMEM((HOSTS, 8, BLOCK), F32),
@@ -612,10 +654,12 @@
             pltpu.VMEM((BLOCKS, BLOCK), F32),
             pltpu.VMEM((HOSTS * SLOTS, BLOCK), F32),
             pltpu.VMEM((QUARTERS, WIDTH, COLS), F32),
-            pltpu.VMEM((QUARTERS, 3, 2 * share + 16, COLS), jnp.int16),
-            pltpu.VMEM((QUARTERS, 3, 2 * share + 16, COLS), jnp.int16),
-            pltpu.VMEM((QUARTERS, 2, share + 16, COLS), jnp.int16),
-            pltpu.VMEM((8, share + 16, COLS), jnp.int16),
+            pltpu.VMEM((QUARTERS, 2, double, BLOCK), jnp.int16),
+            pltpu.VMEM((QUARTERS, 2, double, BLOCK), jnp.int16),
+            pltpu.VMEM((QUARTERS, 2, single, BLOCK), jnp.int16),
+            pltpu.VMEM((QUARTERS, 2, single, BLOCK), jnp.int16),
+            pltpu.VMEM((QUARTERS, 2, single, BLOCK), jnp.int16),
+            pltpu.VMEM((8, single, BLOCK), jnp.int16),
             pltpu.VMEM((2 * share, COLS), F32),
             pltpu.VMEM((QUARTERS, BLOCKS + HOSTS, BLOCK), F32),
             pltpu.VMEM((SLOTS, WIDTH), BF16),
@@ -623,8 +667,8 @@
             dma((2,)),
             dma((13,)),
             dma((13,)),
-            dma((12,)),
-            dma((12,)),
+            dma((24,)),
+            dma((24,)),
             dma((7,)),
             dma((7,)),
             dma((6,)),
@@ -635,8 +679,8 @@
             dma((28,)),
             dma((3,)),
             dma((3,)),
-            dma((12,)),
-            dma((12,)),
+            dma((16,)),
+            dma((16,)),
             dma((8,)),
             dma((8,)),
         ],

time: 108 us -> 93.1 us (0.86)
  Pallas kernels: 104 us -> 90.4 us
    pallas_call x1, Pallas kernels: 104 us -> 90.4 us  [on_device(): pl.pallas_call(kernel, out_shape=(pltpu.VMEM((share, COLS), F32), pltpu.V...]
    unnamed x4 -> x2, local copies, waits for them, and re-layouts: 2.17 us -> 1.26 us
where the time goes in v3:
time: 93.1 us; the launch traced here: 92.9 us
  Pallas kernels  90.4 us (97%)
  between operations  1.28 us (1%)
  local copies, waits for them, and re-layouts  1.26 us (1%)
    pallas_call x1, Pallas kernels, on_device(): pl.pallas_call(kernel, out_shape=(pltpu.VMEM((share, COLS), F32), pltpu.V...  90.4 us

profile of v3, /device:TPU:1, one launch (start us, length us, event | category | flops | bytes accessed | tf_op | source)
XLA Modules:
  0.0 92.9 jit_solution(12569554151246019702)
XLA Ops:
  1.3 90.4 %shard_map.59 = (f32[48,512]{1,0:T(8,128)S(1)}, f32[64,128]{1,0:T(8,128)S(1)}) custom-call(bf16[512,384]{1,0:T(8,128)(2,1)} %bitcast.3, s32[1,1]{1,0:T(1,128)S(6)} %copy.10.counts_ref, s32[1,64]{1,0:T(1,128)} %dest_ref.1, bf16[384,512]{1,0:T(8,128)(2,1)} %cents_hbm.1), custom_call_target="tpu_custom_call" | custom-call | flops 12999999488 | bytes 2000000 | tf_op jit(solution)/shard_map/pallas_call | solution.py:635
  91.7 0.6 copy.8
  92.3 0.6 copy.9

commit v4 on v3

--- a/solution.py
+++ b/solution.py
@@ -125,23 +125,19 @@
     greeted = [along_z(1), along_z(7)]
     greeted += [along_host(step) for step in range(1, 8)]
     greeted += [along_x(step) for step in range(1, 4)]
+    load_docs = pltpu.make_async_copy(docs_hbm, docs_ref, load_sem.at[0])
+    load_cents = pltpu.make_async_copy(cents_hbm, cents_ref, load_sem.at[1])
+    load_docs.start()
+    load_cents.start()
     for other in greeted:
         pl.semaphore_signal(
             barrier, inc=1, device_id=other, device_id_type=pl.DeviceIdType.MESH
         )
-    load_docs = pltpu.make_async_copy(docs_hbm, docs_ref, load_sem.at[0])
-    load_cents = pltpu.make_async_copy(cents_hbm, cents_ref, load_sem.at[1])
-    load_docs.start()
-    load_cents.start()
 
     load_docs.wait()
     values = docs_ref[...].astype(F32)
     factor = lax.rsqrt(jnp.mean(values * values, axis=1, keepdims=True) + 1e-06)
     units[host] = (values * factor * WIDTH ** (-0.5)).astype(BF16)
-    load_cents.wait()
-    values = cents_ref[...].astype(F32)
-    factor = lax.rsqrt(jnp.mean(values * values, axis=0, keepdims=True) + 1e-06)
-    cents[hi] = (values * factor * WIDTH ** (-0.5)).astype(BF16)
     live_counts[host] = jnp.full((8, BLOCK), counts_ref[0, 0].astype(F32), F32)
     col_acc[...] = jnp.zeros_like(col_acc)
 
@@ -248,18 +244,19 @@
     def sides_twin(at):
         return mod(y + 1 + 2 * at, 4) * 2 + 1 - core
 
-    def near(at):
-        return mod(y + 3 + (at >> 1), 4) * 2 + (core ^ (at & 1))
-
-    score_tiles(host, (hi,))
     pl.semaphore_wait(barrier, 12)
 
     for copy in count_copies:
         copy.start()
     give(0, 3, 6)
+    load_cents.wait()
+    values = cents_ref[...].astype(F32)
+    factor = lax.rsqrt(jnp.mean(values * values, axis=0, keepdims=True) + 1e-06)
+    cents[hi] = (values * factor * WIDTH ** (-0.5)).astype(BF16)
     for step in range(8):
         origins[step].start()
     give(1, 2)
+    score_tiles(host, (hi,))
     relay(0)
     for copy in count_copies:
         copy.wait_recv()
@@ -284,32 +281,28 @@
     take(7, 8, 9, 10)
     relay(10)
     score_hosts(2, sides_twin, (hi, relay_quarter), 2)
+    for step in range(4, 8):
+        origins[step].wait_recv()
+    score_hosts(2, here, (other_quarter,), 2)
     relay(11)
     take(4, 5)
     give(11, 12)
-    for step in range(4, 8):
-        origins[step].wait_recv()
-    score_hosts(6, near, (other_quarter,), 3)
+    score_hosts(2, sides, (other_quarter,), 2)
+    score_hosts(2, sides_twin, (other_quarter,), 2)
     score_tiles(across, (hi, relay_quarter, other_quarter))
+    take(11, 12)
+    score_tiles(across ^ 1, (hi, relay_quarter, other_quarter))
     for step in range(8, 12):
         origins[step].wait_recv()
-    score_hosts(6, near, (far_quarter,), 3)
-    take(11, 12)
-    score_tiles(across, (far_quarter,))
-    score_tiles(across ^ 1, (hi, relay_quarter, other_quarter, far_quarter))
-
-    for at in range(13):
-        unit_copies[at].wait_send()
-    for step in range(12):
-        relays[step].wait_send()
-        origins[step].wait_send()
-    for copy in count_copies:
-        copy.wait_send()
-
-    for which in range(HOSTS):
-        for slot in range(MOST):
-            at = which * MOST + slot
-            live[at : at + 1, :] = jnp.where(live_counts[which, 0:1, :] > slot, 1.0, 0.0)
+    score_hosts(8, lambda at: at, (far_quarter,), 4)
+
+    pending = unit_copies + relays + origins + count_copies
+
+    def mask_rows():
+        for which in range(HOSTS):
+            for slot in range(MOST):
+                at = which * MOST + slot
+                live[at : at + 1, :] = jnp.where(live_counts[which, 0:1, :] > slot, 1.0, 0.0)
 
     def exchange_columns(turn):
         for quarter in range(QUARTERS):
@@ -330,8 +323,11 @@
         ]
         for copy in copies:
             copy.start()
+        pending.extend(copies)
+        if turn == 0:
+            mask_rows()
         for copy in copies:
-            copy.wait()
+            copy.wait_recv()
         col_z[turn, z] = (col_x[turn, 0] + col_x[turn, 1]) + (col_x[turn, 2] + col_x[turn, 3])
         copies = [
             remote(
@@ -345,8 +341,9 @@
         ]
         for copy in copies:
             copy.start()
+        pending.extend(copies)
         for copy in copies:
-            copy.wait()
+            copy.wait_recv()
         total = col_z[turn, 0]
         for other in range(1, 8):
             total = total + col_z[turn, other]
@@ -358,7 +355,8 @@
             )
             scale[quarter] = jnp.broadcast_to(line, (8, COLS))
 
-    half_blocks = BLOCKS // 2
+    chunks = 4
+    chunk_blocks = BLOCKS // chunks
 
     def row_pass(turn, half):
         def body(at, _):
@@ -373,20 +371,21 @@
             rows[turn, host, pl.ds(at, 1), :] = jnp.sum(total.T, axis=0, keepdims=True)
             return 0
 
-        lax.fori_loop(half * half_blocks, (half + 1) * half_blocks, body, 0, unroll=4)
-        ref = rows.at[turn, host, pl.ds(half * half_blocks, half_blocks)]
+        lax.fori_loop(half * chunk_blocks, (half + 1) * chunk_blocks, body, 0, unroll=8)
+        ref = rows.at[turn, host, pl.ds(half * chunk_blocks, chunk_blocks)]
         copies = []
         for step in range(1, 8):
-            at = (turn * 2 + half) * 7 + step - 1
+            at = (turn * chunks + half) * 7 + step - 1
             copies.append(remote(ref, ref, row_send.at[at], row_recv.at[at], along_host(step)))
         for copy in copies:
             copy.start()
         return copies
 
     def doc_scales(turn, half, copies):
+        pending.extend(copies)
         for copy in copies:
-            copy.wait()
-        part = slice(half * half_blocks, (half + 1) * half_blocks)
+            copy.wait_recv()
+        part = slice(half * chunk_blocks, (half + 1) * chunk_blocks)
         total = rows[turn, 0, part, :]
         for other in range(1, HOSTS):
             total = total + rows[turn, other, part, :]
@@ -403,11 +402,11 @@
             col_acc[quarter] += jnp.sum(weights.reshape(BLOCK // 8, 8, COLS), axis=0)
         return 0
 
-    sent = [row_pass(0, half) for half in range(2)]
-    for half in range(2):
+    sent = [row_pass(0, half) for half in range(chunks)]
+    for half in range(chunks):
         part, doc_scale = doc_scales(0, half, sent[half])
         doc_row[part, :] = doc_scale * live[part, :]
-        lax.fori_loop(half * half_blocks, (half + 1) * half_blocks, column_body, 0, unroll=4)
+        lax.fori_loop(half * chunk_blocks, (half + 1) * chunk_blocks, column_body, 0, unroll=8)
     exchange_columns(1)
 
     def spread(at, _):
@@ -480,11 +479,11 @@
     def quarter_of(at):
         return mod(hi + (2, 1, 3, 0)[at], QUARTERS)
 
-    def numerators(at, half):
+    def numerators(at, begin, end):
         quarter = quarter_of(at)
         line = scale[quarter][None]
         total = None
-        for which in range(half * HOSTS // 2, (half + 1) * HOSTS // 2):
+        for which in range(begin, end):
             here = slice(which * SLOTS, (which + 1) * SLOTS)
             factor = wide(doc_col[here, :])
             plan = (factor * score[quarter, here, :]).reshape(SLOTS // 8, 8, COLS) * line
@@ -493,7 +492,7 @@
                 units[which], plan, (((0,), (0,)), ((), ())), preferred_element_type=F32
             )
             total = term if total is None else total + term
-        if half == 0:
+        if begin == 0:
             numer[at] = total
         else:
             numer[at] += total
@@ -548,13 +547,13 @@
             encode([reduced[other_half, :]], out_z.at[last, 0])
             all_shares[-1].start()
 
-    sent = [row_pass(1, half) for half in range(2)]
-    for half in range(2):
+    sent = [row_pass(1, half) for half in range(chunks)]
+    for half in range(chunks):
         part, doc_scale = doc_scales(1, half, sent[half])
         doc_log[hi, part, :] = jnp.log(DOCS * doc_scale)
         doc_row[part, :] = DOCS * doc_scale * live[part, :]
-        lax.fori_loop(half * half_blocks, (half + 1) * half_blocks, spread, 0, unroll=4)
-        numerators(0, half)
+        lax.fori_loop(half * chunk_blocks, (half + 1) * chunk_blocks, spread, 0, unroll=8)
+        numerators(0, half * HOSTS // chunks, (half + 1) * HOSTS // chunks)
     for which in range(HOSTS):
         doc_log[hi, BLOCKS + which : BLOCKS + which + 1, :] = live_counts[which, 0:1, :]
     log_copies = [
@@ -572,14 +571,12 @@
 
     for at in range(QUARTERS):
         if at > 0:
-            numerators(at, 0)
-            numerators(at, 1)
+            numerators(at, 0, HOSTS)
+        open_x(at)
         if at >= 2:
             close_x(at - 2)
-        open_x(at)
     close_x(2)
     reduce_x(0)
-    reduce_x(1)
 
     for copy in log_copies:
         copy.wait()
@@ -606,11 +603,12 @@
     )
 
     close_x(3)
+    reduce_x(1)
     reduce_x(2)
     reduce_x(3)
     total = reduced[own_half, :]
-    for step in range(1, 8):
-        other = mod(z + step, 8)
+    for step in range(7, 0, -1):
+        other = mod(z + 8 + (1 - 2 * lo) * step, 8)
         remote(
             in_z.at[other], in_z.at[other], share_send.at[0], share_recv.at[other], along_z(1)
         ).wait_recv()
@@ -620,7 +618,7 @@
     for at in range(QUARTERS):
         for copy in all_sums[at][0] + all_sums[at][1]:
             copy.wait_send()
-    for copy in all_shares:
+    for copy in pending + all_shares:
         copy.wait_send()
 
 
@@ -675,8 +673,8 @@
             dma((6,)),
             dma((14,)),
             dma((14,)),
-            dma((28,)),
-            dma((28,)),
+            dma((56,)),
+            dma((56,)),
             dma((3,)),
             dma((3,)),
             dma((16,)),

time: 93.1 us -> 91.1 us (0.979)
  Pallas kernels: 90.4 us -> 88.5 us
    pallas_call x1, Pallas kernels: 90.4 us -> 88.5 us  [on_device(): pl.pallas_call(kernel, out_shape=(pltpu.VMEM((share, COLS), F32), pltpu.V...]
where the time goes in v4:
time: 91.1 us; the launch traced here: 91 us
  Pallas kernels  88.5 us (97%)
  between operations  1.28 us (1%)
  local copies, waits for them, and re-layouts  1.26 us (1%)
    pallas_call x1, Pallas kernels, on_device(): pl.pallas_call(kernel, out_shape=(pltpu.VMEM((share, COLS), F32), pltpu.V...  88.5 us

profile of v4, /device:TPU:1, one launch (start us, length us, event | category | flops | bytes accessed | tf_op | source)
XLA Modules:
  0.0 91.0 jit_solution(15640603950860311334)
XLA Ops:
  1.3 88.5 %shard_map.59 = (f32[48,512]{1,0:T(8,128)S(1)}, f32[64,128]{1,0:T(8,128)S(1)}) custom-call(bf16[512,384]{1,0:T(8,128)(2,1)} %bitcast.3, s32[1,1]{1,0:T(1,128)S(6)} %copy.10.counts_ref, s32[1,64]{1,0:T(1,128)} %dest_ref.1, bf16[384,512]{1,0:T(8,128)(2,1)} %cents_hbm.1), custom_call_target="tpu_custom_call" | custom-call | flops 12999999488 | bytes 2000000 | tf_op jit(solution)/shard_map/pallas_call | solution.py:633
  89.7 0.6 copy.8
  90.4 0.6 copy.9

commit v5 on v4

--- a/solution.py
+++ b/solution.py
@@ -207,7 +207,7 @@
             count_recv.at[step - 1],
             along_host(step),
         )
-        for step in range(1, 8)
+        for step in (4, 5, 3, 6, 2, 7, 1)
     ]
 
     def take(*numbers):
@@ -298,6 +298,10 @@
 
     pending = unit_copies + relays + origins + count_copies
 
+    def settle():
+        while pending:
+            pending.pop().wait_send()
+
     def mask_rows():
         for which in range(HOSTS):
             for slot in range(MOST):
@@ -319,7 +323,7 @@
                 colx_recv.at[turn * 3 + step - 1],
                 along_x(step),
             )
-            for step in range(1, 4)
+            for step in (2, 1, 3)
         ]
         for copy in copies:
             copy.start()
@@ -337,10 +341,11 @@
                 colz_recv.at[turn * 7 + step - 1],
                 along_z(step),
             )
-            for step in range(1, 8)
+            for step in (4, 3, 5, 2, 6, 1, 7)
         ]
         for copy in copies:
             copy.start()
+        settle()
         pending.extend(copies)
         for copy in copies:
             copy.wait_recv()
@@ -355,8 +360,8 @@
             )
             scale[quarter] = jnp.broadcast_to(line, (8, COLS))
 
-    chunks = 4
-    chunk_blocks = BLOCKS // chunks
+    bounds = ((0, 8), (8, 16), (16, 24), (24, 32))
+    chunks = len(bounds)
 
     def row_pass(turn, half):
         def body(at, _):
@@ -371,10 +376,10 @@
             rows[turn, host, pl.ds(at, 1), :] = jnp.sum(total.T, axis=0, keepdims=True)
             return 0
 
-        lax.fori_loop(half * chunk_blocks, (half + 1) * chunk_blocks, body, 0, unroll=8)
-        ref = rows.at[turn, host, pl.ds(half * chunk_blocks, chunk_blocks)]
+        lax.fori_loop(*bounds[half], body, 0, unroll=8)
+        ref = rows.at[turn, host, pl.ds(bounds[half][0], bounds[half][1] - bounds[half][0])]
         copies = []
-        for step in range(1, 8):
+        for step in (4, 5, 3, 6, 2, 7, 1):
             at = (turn * chunks + half) * 7 + step - 1
             copies.append(remote(ref, ref, row_send.at[at], row_recv.at[at], along_host(step)))
         for copy in copies:
@@ -385,7 +390,7 @@
         pending.extend(copies)
         for copy in copies:
             copy.wait_recv()
-        part = slice(half * chunk_blocks, (half + 1) * chunk_blocks)
+        part = slice(*bounds[half])
         total = rows[turn, 0, part, :]
         for other in range(1, HOSTS):
             total = total + rows[turn, other, part, :]
@@ -406,7 +411,7 @@
     for half in range(chunks):
         part, doc_scale = doc_scales(0, half, sent[half])
         doc_row[part, :] = doc_scale * live[part, :]
-        lax.fori_loop(half * chunk_blocks, (half + 1) * chunk_blocks, column_body, 0, unroll=8)
+        lax.fori_loop(*bounds[half], column_body, 0, unroll=8)
     exchange_columns(1)
 
     def spread(at, _):
@@ -552,31 +557,38 @@
         part, doc_scale = doc_scales(1, half, sent[half])
         doc_log[hi, part, :] = jnp.log(DOCS * doc_scale)
         doc_row[part, :] = DOCS * doc_scale * live[part, :]
-        lax.fori_loop(half * chunk_blocks, (half + 1) * chunk_blocks, spread, 0, unroll=8)
-        numerators(0, half * HOSTS // chunks, (half + 1) * HOSTS // chunks)
-    for which in range(HOSTS):
-        doc_log[hi, BLOCKS + which : BLOCKS + which + 1, :] = live_counts[which, 0:1, :]
-    log_copies = [
-        remote(
-            doc_log.at[hi],
-            doc_log.at[hi],
-            log_send.at[step - 1],
-            log_recv.at[step - 1],
-            along_z(2 * step),
-        )
-        for step in range(1, 4)
-    ]
-    for copy in log_copies:
-        copy.start()
+        lax.fori_loop(*bounds[half], spread, 0, unroll=8)
+        numerators(0, bounds[half][0] // MOST, bounds[half][1] // MOST)
+    log_copies = []
+
+    def send_logs():
+        for which in range(HOSTS):
+            doc_log[hi, BLOCKS + which : BLOCKS + which + 1, :] = live_counts[which, 0:1, :]
+        copies = [
+            remote(
+                doc_log.at[hi],
+                doc_log.at[hi],
+                log_send.at[step - 1],
+                log_recv.at[step - 1],
+                along_z(2 * step),
+            )
+            for step in range(1, 4)
+        ]
+        for copy in copies:
+            copy.start()
+        log_copies.extend(copies)
 
     for at in range(QUARTERS):
         if at > 0:
             numerators(at, 0, HOSTS)
         open_x(at)
+        if at == 0:
+            send_logs()
         if at >= 2:
             close_x(at - 2)
     close_x(2)
     reduce_x(0)
+    settle()
 
     for copy in log_copies:
         copy.wait()
@@ -618,7 +630,7 @@
     for at in range(QUARTERS):
         for copy in all_sums[at][0] + all_sums[at][1]:
             copy.wait_send()
-    for copy in pending + all_shares:
+    for copy in all_shares:
         copy.wait_send()
 
 

time: 91.1 us -> 90.5 us (level)
  no operation moved by 1% of the time
where the time goes in v5:
time: 90.5 us; the launch traced here: 90.3 us
  Pallas kernels  87.8 us (97%)
  between operations  1.28 us (1%)
  local copies, waits for them, and re-layouts  1.26 us (1%)
    pallas_call x1, Pallas kernels, on_device(): pl.pallas_call(kernel, out_shape=(pltpu.VMEM((share, COLS), F32), pltpu.V...  87.8 us

profile of v5, /device:TPU:1, one launch (start us, length us, event | category | flops | bytes accessed | tf_op | source)
XLA Modules:
  0.0 90.3 jit_solution(14067830791187278166)
XLA Ops:
  1.3 87.8 %shard_map.59 = (f32[48,512]{1,0:T(8,128)S(1)}, f32[64,128]{1,0:T(8,128)S(1)}) custom-call(bf16[512,384]{1,0:T(8,128)(2,1)} %bitcast.3, s32[1,1]{1,0:T(1,128)S(6)} %copy.10.counts_ref, s32[1,64]{1,0:T(1,128)} %dest_ref.1, bf16[384,512]{1,0:T(8,128)(2,1)} %cents_hbm.1), custom_call_target="tpu_custom_call" | custom-call | flops 12999999488 | bytes 2000000 | tf_op jit(solution)/shard_map/pallas_call | solution.py:645
  89.1 0.6 copy.8
  89.7 0.6 copy.9
